TPU v7x, 32 devices: a whole 2x2x4 slice. The times are simulated.
32 devices in a mesh: dp: 8 (over z, y), pipe: 4 (over x, core).
Axes of the slice: x: 2, y: 2, z: 4, core: 2. Of those that a mesh axis runs over, the one named last changes fastest.
Arguments:
- frames: bfloat16 [32, 8, 3, 8, 64], P('dp'), may hold values from -40 to 40
- cut_mask: int32 [32, 7], P('dp'), may hold values 0 or 1
- offsets: int32 [32], P('dp'), may hold values from 2 to 6
- stem_kernel: bfloat16 [147, 64], replicated, may hold values from -0.5 to 0.5
- diff_kernel: bfloat16 [9, 6, 64], replicated, may hold values from -0.875 to 0.875
- stem_gain: float32 [64], replicated, may hold values from 0.1 to 1.9
- stem_bias: float32 [64], replicated, may hold values from -4 to 4
- reduce_weight: bfloat16 [2048, 512], replicated, may hold values from -0.125 to 0.125
- reduce_gain: float32 [512], replicated, may hold values from 0.1 to 1.9
- reduce_bias: float32 [512], replicated, may hold values from -4 to 4
- squeeze_weight: bfloat16 [512, 32], replicated, may hold values from -0.25 to 0.25
- fine_kernel: bfloat16 [9, 32, 32], replicated, may hold values from -0.375 to 0.375
- coarse_kernel: bfloat16 [9, 32, 32], replicated, may hold values from -0.375 to 0.375
- excite_weight: bfloat16 [32, 512], replicated, may hold values from -1 to 1
- middle_kernel: bfloat16 [9, 512, 512], replicated, may hold values from -0.09375 to 0.09375
- expand_weight: bfloat16 [512, 2048], replicated, may hold values from -0.25 to 0.25
- expand_gain: float32 [2048], replicated, may hold values from 0.1 to 1.9
- expand_bias: float32 [2048], replicated, may hold values from -4 to 4
- cotangent: bfloat16 [32, 8, 2, 8, 2048], P('dp'), may hold values from -6 to 6
Outputs:
- frame_grad: float32 [32, 8, 3, 8, 64], P(('dp', 'pipe'))
- stem_kernel_grad: float32 [147, 64], replicated
- diff_kernel_grad: float32 [9, 6, 64], replicated
- stem_gain_grad: float32 [64], replicated
- stem_bias_grad: float32 [64], replicated
- reduce_weight_grad: float32 [2048, 512], replicated
- reduce_gain_grad: float32 [512], replicated
- reduce_bias_grad: float32 [512], replicated
- squeeze_weight_grad: float32 [512, 32], replicated
- fine_kernel_grad: float32 [9, 32, 32], replicated
- coarse_kernel_grad: float32 [9, 32, 32], replicated
- excite_weight_grad: float32 [32, 512], replicated
- middle_kernel_grad: float32 [9, 512, 512], replicated
- expand_weight_grad: float32 [512, 2048], replicated
- expand_gain_grad: float32 [2048], replicated
- expand_bias_grad: float32 [2048], replicated
Inputs may be any that keep to these rules, and one draw needn't show every extreme that they name: Each clip holds two videos, of offsets[c] and 8 - offsets[c] frames.
All inputs are finite; a program needn't handle non-finite values. No bound on the sum of `cut_mask` on one device may be relied on, other than what follows from the above.
Results may differ from a plain program's by a relative error of at most 0.02.
Values may be sent and summed in bfloat16 or wider, within the bound.
No kernel may reach another device: no remote copies, remote signals or barrier semaphores. Data moves between devices by JAX's collectives and lax.ppermute only.
A program may use at most 256 MiB of HBM per device.

v0:
```python
import functools

import jax
import jax.numpy as jnp
from jax import lax
from jax.experimental import pallas as pl
from jax.experimental.pallas import tpu as pltpu
from jax.sharding import PartitionSpec as P

FRAMES = 8
MICRO = 4
EPSILON = 1e-05
COST = 1_000_000
ORDER = (
    ("K", "R", "Ma", "St", "Rs", "Mb", "O", "Mc", "Oa", "Z", "Md", "B", "Ob", "Mn", "Oc", "Od")
    + ("T0", "Mf", "T3", "On", "F", "T4", "G")
)
FINISH_BYTES = 16 * 1024 * 1024
VMEM_BYTES = 32 * 1024 * 1024
BF = jnp.bfloat16
F32 = jnp.float32

STEM = 64
SLOT = 16


def dot(left, right):
    return jnp.dot(left, right, preferred_element_type=F32)


def dot_nt(left, right):
    return lax.dot_general(left, right, (((1,), (1,)), ((), ())), preferred_element_type=F32)


def dot_tn(left, right):
    return lax.dot_general(left, right, (((0,), (0,)), ((), ())), preferred_element_type=F32)


def dot_exact(left, right):
    return jnp.dot(left, right, preferred_element_type=F32, precision=lax.Precision.HIGHEST)


def iota(shape, dim):
    return lax.broadcasted_iota(jnp.int32, shape, dim)


def sigmoid(v):
    return 1.0 / (1.0 + jnp.exp(-v))


def swish_slope(v):
    s = sigmoid(v)
    return s * (1.0 + v * (1.0 - s))


def keep_column(pack, lanes):
    rows = pack[192:208, :].astype(F32)
    return jnp.concatenate(
        [jnp.broadcast_to(rows[f : f + 1, :lanes], (8, lanes)) for f in range(FRAMES)], 0
    )


def gate_column(pack):
    keep = keep_column(pack, 64)
    both = jnp.concatenate([keep, keep], 1)
    return jnp.concatenate([jnp.zeros((8, 128), F32), both[:-8]], 0)


def pack_clip(place, cut, offset, frames, out):
    clip = place[0]
    row = cut[pl.ds(clip, 1), :]
    own = iota((1, MICRO), 1) == clip
    stop = jnp.sum(jnp.where(own, offset[...], 0), 1, keepdims=True)
    step = iota(row.shape, 1)
    valid = jnp.where(step + 1 == stop, 0, row).astype(F32)
    spread = iota((16, FRAMES - 1), 0) == iota((16, FRAMES - 1), 1)
    column = jnp.sum(jnp.where(spread, valid, 0.0), 1, keepdims=True)
    out[0:192, :] = frames[...].astype(F32).reshape(192, 64).astype(BF)
    out[192:208, :] = jnp.broadcast_to(column, (16, 64)).astype(BF)


def summed_up(pieces):
    value = pieces[0][...]
    for piece in pieces[1:]:
        value = value + piece[...]
    return value


def spread_sums(out, first, second):
    out[...] = jnp.concatenate([first, second], 0)


def norm_scale(sums, row_total):
    mean = sums[0:1] * (1.0 / row_total)
    variance = sums[1:2] * (1.0 / row_total) - mean * mean
    return mean, lax.rsqrt(variance + EPSILON)


def column_sums(out, first, second):
    spread_sums(out, jnp.sum(first, 0, keepdims=True), jnp.sum(second, 0, keepdims=True))


def fold_lanes(sums):
    for step in (64, 128, 256):
        sums = sums + pltpu.roll(sums, step, 1)
    return sums


def shift_rows(v, dy, dx):
    rows = v.shape[0]
    if dx:
        rolled = pltpu.roll(v, (-dx) % rows, 0)
        wb = lax.rem(iota(v.shape, 0), 8)
        v = jnp.where((wb + dx >= 0) & (wb + dx < 8), rolled, 0.0)
    half = rows // 2
    if dy == 1:
        v = jnp.concatenate([v[half:], jnp.zeros_like(v[half:])], 0)
    elif dy == -1:
        v = jnp.concatenate([jnp.zeros_like(v[:half]), v[:half]], 0)
    return v


def cell_sum(v):
    half = v.shape[0] // 2
    both = v[:half] + v[half:]
    even = lax.rem(iota(both.shape, 0), 2) == 0
    both = both + jnp.where(even, pltpu.roll(both, half - 1, 0), pltpu.roll(both, 1, 0))
    return jnp.concatenate([both, both], 0)


def taps(v):
    return [shift_rows(v, ky - 1, kx - 1) for ky in range(3) for kx in range(3)]


def back_taps(v):
    return [shift_rows(v, 1 - ky, 1 - kx) for ky in range(3) for kx in range(3)]


def coarse_taps(v):
    return [shift_rows(v, 0, 2 * (k - 1)) for k in range(3)]


def window_select(rows, cols, kind):
    place = iota((rows, cols), 0)
    col = iota((rows, cols), 1)
    lane = lax.rem(place, 128)
    tap_row = lax.div(place, 128)
    channel = lax.div(lane, SLOT)
    slot = lax.rem(lane, SLOT)
    if kind == "stem":
        hit = (col == (7 * tap_row + slot) * 3 + channel) & (slot < 7) & (channel < 3)
        return jnp.where(hit, 1.0, 0.0)
    cell = lax.div(slot - 1, 2)
    hit = (col == (3 * tap_row + cell) * 6 + channel) & (slot >= 1) & (slot < 7) & (channel < 6)
    return jnp.where(hit, 0.25, 0.0)


def spread_select():
    w = iota((64, 128), 0)
    lane = iota((64, 128), 1)
    return jnp.where(w == 8 * lax.div(lane, SLOT) + lax.rem(lane, SLOT) - 3, 1.0, 0.0)


def gather_select():
    row = iota((384, 128), 0)
    col = iota((384, 128), 1)
    return jnp.where(col == lax.div(row, 128) * SLOT + lax.rem(row, SLOT), 1.0, 0.0)


def own_block():
    row = iota((8, 128), 0)
    lane = iota((8, 128), 1)
    return jnp.where(lax.div(lane, SLOT) == row, 1.0, 0.0)


def stem_windows(pack, kernel, diff, win, win2, u, u2, spread, tiles):
    spread[...] = dot(pack[0:192, :], spread_select().astype(BF))
    mask = own_block()
    for f in range(8):
        for c in range(3):
            for h in range(8):
                line = f * 24 + c * 8 + h
                tiles[h * 64 + f * 8 : h * 64 + f * 8 + 8, c * 128 : c * 128 + 128] = (
                    jnp.broadcast_to(spread[line : line + 1, :], (8, 128)) * mask
                )
    pixels = dot(tiles[...].astype(BF), gather_select().astype(BF))
    rows = [pixels[64 * h : 64 * h + 64] for h in range(8)]
    gate = gate_column(pack)
    steps = []
    for h2 in range(4):
        both = rows[2 * h2] + rows[2 * h2 + 1]
        step = (both - jnp.concatenate([jnp.zeros((8, 128), F32), both[:-8]], 0)) * gate
        later = jnp.concatenate([step[8:], jnp.zeros((8, 128), F32)], 0)
        steps.append((step + pltpu.roll(later, 48, 1)).astype(BF))
    rows = [r.astype(BF) for r in rows]
    blank = jnp.zeros((64, 128), BF)
    for dy in range(7):
        for h in range(8):
            source = h + dy - 3
            win[64 * h : 64 * h + 64, 128 * dy : 128 * dy + 128] = (
                rows[source] if 0 <= source < 8 else blank
            )
    for dy in range(3):
        for h in range(4):
            source = h + dy - 1
            win2[64 * h : 64 * h + 64, 128 * dy : 128 * dy + 128] = (
                steps[source] if 0 <= source < 4 else blank
            )
    low_half = iota((896, 128), 1) < 64
    wide_kernel = jnp.concatenate([kernel[...], kernel[...]], 0)
    placed = dot_nt(window_select(896, 147, "stem").astype(BF), wide_kernel)
    taps = diff[...].astype(F32)
    rows = jnp.concatenate([taps[k] for k in range(9)], 0)
    wide_diff = jnp.concatenate([rows, rows], 1).astype(BF)
    placed2 = dot(window_select(384, 54, "diff").astype(BF), wide_diff)
    for q in range(4):
        first = pltpu.roll(placed, 2 * q, 0) if q else placed
        second = pltpu.roll(placed, 2 * q + 1, 0)
        u[:, 128 * q : 128 * q + 128] = jnp.where(low_half, first, second).astype(BF)
        u2[:, 128 * q : 128 * q + 128] = (
            pltpu.roll(placed2, 2 * q, 0) if q else placed2
        ).astype(BF)


class Pick:
    def __init__(self, info, own, other):
        self.stays = info[info.shape[0] - 1] == 1
        self.own, self.other = own, other

    def __getitem__(self, place):
        return jnp.where(self.stays, self.own[place], self.other[place])


def stem_front(
    info, pack, kernel, diff, v_out, sums_out, win, win2, u, u2, spread, tiles
):
    stem_windows(Pick(info, *pack), kernel, diff, win, win2, u, u2, spread, tiles)
    v = dot(win[...], u[...])
    side = dot(win2[...], u2[...])
    first = jnp.zeros((1, 512), F32)
    second = jnp.zeros((1, 512), F32)
    for h in range(8):
        piece = v[64 * h : 64 * h + 64] + side[64 * (h // 2) : 64 * (h // 2) + 64]
        v_out[64 * h : 64 * h + 64, :] = piece
        first = first + jnp.sum(piece, 0, keepdims=True)
        second = second + jnp.sum(piece * piece, 0, keepdims=True)
    spread_sums(sums_out, first, second)


def stem_close(
    row_total, info, v, sums, gain, bias, weight, wide_out, keep_out, send_out, red_out, sums_out,
    save,
):
    mean, scale = norm_scale(fold_lanes(summed_up(sums)), row_total)
    save[512:513, :] = scale
    for h in range(8):
        normal = (v[64 * h : 64 * h + 64, :] - mean) * scale
        save[64 * h : 64 * h + 64, :] = normal
        y = normal * gain[...] + bias[...]
        wide_out[
            64 * (h // 4) : 64 * (h // 4) + 64, 512 * (h % 4) : 512 * (h % 4) + 512
        ] = (y * sigmoid(y)).astype(BF)
    save.flush()
    wide_out.flush()
    keep_out[...] = wide_out[:, lanes(1024 * info[0], 1024)]
    send_out[...] = wide_out[:, lanes(1024 * (1 - info[0]), 1024)]
    red = dot(wide_out[...], weight[...])
    red_out[...] = red
    column_sums(sums_out, red, red * red)


def gate_path(pack, narrow, squeeze, fine, coarse, excite):
    squeezed = dot_nt(narrow.astype(BF), squeeze[...])
    keep = keep_column(pack, 32)
    parts = []
    for hb in range(2):
        part = squeezed[64 * hb : 64 * hb + 64]
        later = jnp.concatenate([part[8:], part[:8]], 0)
        parts.append((later - part) * keep)
    change = jnp.concatenate(parts, 0)
    fine_rows = jnp.concatenate(taps(change), 1).astype(BF)
    pooled = 0.25 * cell_sum(change)
    coarse_rows = jnp.concatenate(coarse_taps(pooled), 1).astype(BF)
    summed = (dot(fine_rows, fine[...]) + dot(coarse_rows, coarse[96:192, :])).astype(BF)
    return fine_rows, coarse_rows, summed, sigmoid(dot(summed, excite[...]))


def gate_front(
    row_total, info, red, sums, pack, gain, bias, squeeze, fine, coarse, excite, middle, expand,
    keep_out, send_out, exp_out, sums_out, save, both,
):
    mean, scale = norm_scale(summed_up(sums), row_total)
    normal = (red[...] - mean) * scale
    save[0:128, :] = normal
    save[128:129, :] = scale
    save.flush()
    y = normal * gain[...] + bias[...]
    narrow = y * sigmoid(y)
    gate = gate_path(pack, narrow, squeeze, fine, coarse, excite)[3]
    gated = narrow * (1.0 + gate)
    total = jnp.zeros((128, 512), F32)
    for k, piece in enumerate(taps(gated)):
        total = total + dot(piece.astype(BF), middle[k])
    save[136:264, :] = total
    save.flush()
    hidden = (total * sigmoid(total)).astype(BF)
    for half in range(2):
        part = slice(256 * half, 256 * half + 256)
        both[:, 512 * half : 512 * half + 256] = gated[:, part].astype(BF)
        both[:, 512 * half + 256 : 512 * half + 512] = hidden[:, part]
    keep_out[...] = both[:, lanes(512 * info[0], 512)]
    send_out[...] = both[:, lanes(512 * (1 - info[0]), 512)]
    expanded = dot(hidden, expand[...])
    exp_out[...] = expanded
    column_sums(sums_out, expanded, expanded * expanded)


def out_back(row_total, expanded, sums, gain, bias, wide, cot, sums_out, save):
    mean, scale = norm_scale(summed_up(sums), row_total)
    save[256:257, :] = scale
    first = jnp.zeros((1, 2048), F32)
    second = jnp.zeros((1, 2048), F32)
    for hb in range(2):
        part = slice(64 * hb, 64 * hb + 64)
        if hb:
            save.flush()
            save.flush()
        normal = (expanded[part, :] - mean) * scale
        y = normal * gain[...] + bias[...] + wide[part, :].astype(F32)
        weightless = cot[:, hb, :, :].astype(F32).reshape(64, 2048)
        og = weightless * swish_slope(y)
        save[part, :] = og
        save[128 + 64 * hb : 192 + 64 * hb, :] = normal
        first = first + jnp.sum(og, 0, keepdims=True)
        second = second + jnp.sum(og * normal, 0, keepdims=True)
    spread_sums(sums_out, first, second)


def norm_pull(grad, normal, scale, gain, grad_sums, row_total):
    return (
        gain
        * scale
        * (
            grad
            - grad_sums[0:1] * (1.0 / row_total)
            - normal * (grad_sums[1:2] * (1.0 / row_total))
        )
    )


def block_order(info, partner=False):
    block = 2 * info[1] + info[2]
    first = jnp.where((info[0] == 0) != partner, 2, 1)
    return [block, block ^ first, block ^ (3 - first), block ^ 3]


def lanes(start, width):
    return pl.ds(pl.multiple_of(start, 128), width)


def expand_back(
    row_total, info, grad_sums, saved, hpre, gain, expand, hg_out, total_out, *rest
):
    outs, (hg_scratch, dv_scratch) = rest[:4], rest[4:]
    sums = summed_up(grad_sums)
    total_out[0:2, :] = sums
    total_out.flush()
    dv = norm_pull(
        saved[0:128, :], saved[128:256, :], saved[256:257, :], gain[...], sums, row_total
    ).astype(BF)
    dv_scratch[...] = dv
    dhid = dot_nt(dv, expand[...]).astype(BF).astype(F32)
    hg = (dhid * swish_slope(hpre[...])).astype(BF)
    hg_out[...] = hg
    hg_scratch[...] = hg
    for out, block in zip(outs, block_order(info)):
        out[:, :128] = hg_scratch[:, lanes(128 * block, 128)]
        out[:, 128:] = dv_scratch[:, lanes(512 * block, 512)]


def all_rows(refs):
    return jnp.concatenate([ref[...] for ref in refs], 0)


def clip_rows(mine, pair, columns):
    rows = []
    for k, other in enumerate((0, 2, 1, 3)):
        rows.append(mine[128 * k : 128 * k + 128, columns])
        rows.append(pair[128 * other : 128 * other + 128, columns])
    return rows


def depth_halves(info, bit, scratch, keep_out, send_out):
    rows = keep_out.shape[0]
    mine = info[bit]
    keep_out[...] = scratch[pl.ds(pl.multiple_of(mine * rows, 16), rows), :]
    send_out[...] = scratch[pl.ds(pl.multiple_of((1 - mine) * rows, 16), rows), :]


def add_halves(bit, info, keep, got, keep_out, send_out, scratch):
    scratch[...] = (keep[...].astype(F32) + got[...].astype(F32)).astype(BF)
    depth_halves(info, bit, scratch, keep_out, send_out)


def add_rows(keep, got, out):
    out[...] = (keep[...].astype(F32) + got[...].astype(F32)).astype(BF)


def join_halves(bit, info, own, got, out):
    rows = own.shape[0]
    mine = info[bit]
    out[pl.ds(pl.multiple_of(mine * rows, 16), rows), :] = own[...]
    out[pl.ds(pl.multiple_of((1 - mine) * rows, 16), rows), :] = got[...]


def middle_weights(info, left_refs, right_refs, *rest):
    outs, (scratch,) = rest[:-1], rest[-1:]
    left = jnp.concatenate([ref[:, :256] for ref in left_refs], 0).T
    clips = [
        back_taps(rows.astype(F32)) for rows in clip_rows(*right_refs, slice(0, 128))
    ]
    for k in range(9):
        right = jnp.concatenate([clip[k] for clip in clips], 0).astype(BF)
        scratch[256 * k : 256 * k + 256, :] = dot(left, right).astype(BF)
    if scratch.shape[0] > 2304:
        scratch[2304:, :] = jnp.zeros((scratch.shape[0] - 2304, 128), BF)
    depth_halves(info, 3, scratch, *outs)


def outer_weights(info, left_refs, right_refs, wide, late, *rest):
    outs, (scratch,) = rest[:-1], rest[-1:]
    left = jnp.concatenate([ref[:, 256:] for ref in left_refs], 0)
    right = jnp.concatenate(clip_rows(*right_refs, slice(128, 640)), 0)
    result = dot_tn(left, right).astype(BF)
    for q in range(4):
        scratch[256 * q : 256 * q + 256, :] = result[:, 128 * q : 128 * q + 128]
    right = jnp.concatenate(clip_rows(*late, slice(0, 128)), 0)
    scratch[1024:2048, :] = dot_tn(all_rows(wide), right).astype(BF)
    small = [late[0][128 * k : 128 * k + 128, 128:].astype(F32) for k in range(4)]
    scratch[2048:2176, :] = sum(small).astype(BF)
    if scratch.shape[0] > 2176:
        scratch[2176:, :] = jnp.zeros((scratch.shape[0] - 2176, 128), BF)
    depth_halves(info, 3, scratch, *outs)


def copy_rows(source, out):
    out[...] = source[...]


def add_floats(first, second, out):
    out[...] = first[...] + second[...]


def stack_rows(*refs):
    out = refs[-1]
    start = 0
    for ref in refs[:-1]:
        out[start : start + ref.shape[0], :] = ref[...]
        start += ref.shape[0]


def gate_back(
    pack, hg, normal, gain, bias, squeeze, fine, coarse, excite, middle,
    rg_out, sums_out, small_out,
):
    y = normal[...] * gain[...] + bias[...]
    narrow_v = y * sigmoid(y)
    fine_rows, coarse_rows, summed, gate_v = gate_path(
        pack, narrow_v, squeeze, fine, coarse, excite
    )
    total = jnp.zeros((128, 512), F32)
    for k, piece in enumerate(back_taps(hg[...].astype(F32))):
        total = total + dot_nt(piece.astype(BF), middle[k])
    gg = total.astype(BF).astype(F32)
    narrow_grad = gg * (1.0 + gate_v)
    excite_grad = (gg * narrow_v * gate_v * (1.0 - gate_v)).astype(BF)
    dexcite = dot_tn(summed, excite_grad)
    summed_low = dot_nt(excite_grad, excite[...]).astype(BF)
    summed_grad = summed_low.astype(F32)
    coarse_low = cell_sum(summed_grad).astype(BF)
    dfine = dot_tn(fine_rows, summed_low)
    dcoarse = 0.25 * dot_tn(coarse_rows, coarse_low)
    spread = dot_nt(summed_low, fine[...])
    change_grad = jnp.zeros((128, 32), F32)
    for k in range(9):
        change_grad = change_grad + shift_rows(
            spread[:, 32 * k : 32 * k + 32], 1 - k // 3, 1 - k % 3
        )
    spread = dot_nt(coarse_low, coarse[96:192, :])
    pooled_grad = jnp.zeros((128, 32), F32)
    for k in range(3):
        pooled_grad = pooled_grad + shift_rows(spread[:, 32 * k : 32 * k + 32], 0, 2 * (1 - k))
    change_grad = change_grad + 0.25 * pooled_grad
    keep = keep_column(pack, 32)
    parts = []
    for hb in range(2):
        step = change_grad[64 * hb : 64 * hb + 64] * keep
        earlier = jnp.concatenate([step[56:], step[:56]], 0)
        parts.append(earlier - step)
    squeezed_grad = jnp.concatenate(parts, 0).astype(BF)
    dsqueeze = dot_tn(squeezed_grad, narrow_v.astype(BF))
    narrow_grad = narrow_grad + dot(squeezed_grad, squeeze[...])
    rg = narrow_grad * swish_slope(y)
    rg_out[...] = rg
    column_sums(sums_out, rg, rg * normal[...])
    small_out[0:32, :] = dsqueeze[:, :256]
    small_out[32:64, :] = dsqueeze[:, 256:]
    small_out[64:96, :] = dexcite[:, :256]
    small_out[96:128, :] = dexcite[:, 256:]
    pieces = [dfine[32 * k : 32 * k + 32] for k in range(9)]
    pieces += [dcoarse[32 * k : 32 * k + 32] for k in range(3)]
    small_out[128:160, :] = jnp.concatenate(pieces[:8], 1)
    small_out[160:192, :] = jnp.concatenate(pieces[8:] + [jnp.zeros((32, 128), F32)], 1)
    small_out[192:256, :] = jnp.zeros((64, 256), F32)


def reduce_back(
    row_total, info, small, rg, grad_sums, saved, gain, og, weight, stem_saved, stem_gain,
    stem_bias, rs_out, sums_out, total_out, dv0, dv1, dv2, dv3, dv_scratch,
):
    sums = summed_up(grad_sums)
    total_out[0:2, :] = sums
    total_out.flush()
    dv = norm_pull(
        rg[...], saved[0:128, :], saved[128:129, :], gain[...], sums, row_total
    ).astype(BF)
    dv_scratch[...] = dv
    for out, block in zip((dv0, dv1, dv2, dv3), block_order(info)):
        out[:, :128] = dv_scratch[:, lanes(128 * block, 128)]
        part = small[pl.ds(pl.multiple_of(64 * block, 64), 64), :].astype(BF)
        out[:64, 128:] = part[:, :128]
        out[64:, 128:] = part[:, 128:]
    wide_grad = dot_nt(dv, weight[...]) + og[...].astype(BF).astype(F32)
    wide_grad = wide_grad.astype(BF).astype(F32)
    first = jnp.zeros((1, 512), F32)
    second = jnp.zeros((1, 512), F32)
    for h in range(8):
        normal = stem_saved[64 * h : 64 * h + 64, :]
        y = normal * stem_gain[...] + stem_bias[...]
        rs = (
            wide_grad[64 * (h // 4) : 64 * (h // 4) + 64, 512 * (h % 4) : 512 * (h % 4) + 512]
            * swish_slope(y)
        )
        rs_out[64 * h : 64 * h + 64, :] = rs
        first = first + jnp.sum(rs, 0, keepdims=True)
        second = second + jnp.sum(rs * normal, 0, keepdims=True)
    spread_sums(sums_out, first, second)


def stem_back(
    stem_total, share, pack, kernel, diff, saved, gain, rs, grad_sums, og_total,
    rg_total, frames_out, tail_out, win, win2, u, u2, lines, tiles,
):
    stem_windows(pack, kernel, diff, win, win2, u, u2, lines, tiles)
    scale = saved[512:513, :]
    totals = fold_lanes(summed_up(grad_sums))
    rows = []
    pairs = []
    for h in range(8):
        part = slice(64 * h, 64 * h + 64)
        normal = saved[part, :]
        pre = norm_pull(rs[part, :], normal, scale, gain[...], totals, stem_total)
        rows.append(pre.astype(BF))
        if h % 2:
            pairs.append((before + pre).astype(BF))
        before = pre
    dv = jnp.concatenate(rows, 0)
    dside = jnp.concatenate(pairs, 0)

    low_half = iota((896, 128), 1) < 64
    du = dot_tn(win[...], dv)
    placed = jnp.zeros((896, 128), F32)
    for q in range(4):
        part = du[:, 128 * q : 128 * q + 128]
        first = pltpu.roll(part, 896 - 2 * q, 0) if q else part
        placed = placed + jnp.where(low_half, first, pltpu.roll(part, 896 - 2 * q - 1, 0))
    placed = placed + pltpu.roll(placed, 64, 1)
    tail_out[0:147, 0:64] = lax.dot_general(
        window_select(896, 147, "stem"), placed, (((0,), (0,)), ((), ())),
        preferred_element_type=F32, precision=lax.Precision.HIGHEST,
    )[:, :64]
    du2 = dot_tn(win2[...], dside)
    placed = jnp.zeros((384, 128), F32)
    for q in range(4):
        part = du2[:, 128 * q : 128 * q + 128]
        placed = placed + (pltpu.roll(part, 384 - 2 * q, 0) if q else part)
    placed = placed + pltpu.roll(placed, 64, 1)
    tail_out[0:54, 64:128] = lax.dot_general(
        window_select(384, 54, "diff"), placed, (((0,), (0,)), ((), ())),
        preferred_element_type=F32, precision=lax.Precision.HIGHEST,
    )[:, :64]

    dwin = dot_nt(dv, u[...])
    dwin2 = dot_nt(dside, u2[...])
    gate = gate_column(pack)
    steps = []
    for h2 in range(4):
        total = jnp.zeros((64, 128), F32)
        for dy in range(3):
            target = h2 + 1 - dy
            if 0 <= target < 4:
                total = total + dwin2[64 * target : 64 * target + 64, 128 * dy : 128 * dy + 128]
        later = pltpu.roll(total, 80, 1)
        later = jnp.concatenate([jnp.zeros((8, 128), F32), later[:-8]], 0)
        step = (total + later) * gate
        steps.append(step - jnp.concatenate([step[8:], jnp.zeros((8, 128), F32)], 0))
    pixels = []
    for h in range(8):
        total = steps[h // 2]
        for dy in range(7):
            target = h + 3 - dy
            if 0 <= target < 8:
                total = total + dwin[64 * target : 64 * target + 64, 128 * dy : 128 * dy + 128]
        pixels.append(total)
    pixels = jnp.concatenate(pixels, 0)
    back = lax.dot_general(
        pixels, gather_select(), (((1,), (1,)), ((), ())),
        preferred_element_type=F32, precision=lax.Precision.HIGHEST,
    )
    mask = own_block()
    for f in range(8):
        for c in range(3):
            for h in range(8):
                line = f * 24 + c * 8 + h
                block = back[h * 64 + f * 8 : h * 64 + f * 8 + 8, c * 128 : c * 128 + 128]
                lines[line : line + 1, :] = jnp.sum(block * mask, 0, keepdims=True)
    flat = lax.dot_general(
        lines[...], spread_select(), (((1,), (1,)), ((), ())),
        preferred_element_type=F32, precision=lax.Precision.HIGHEST,
    )
    frames_out[...] = flat.reshape(8, 3, 8, 64)
    og_all = og_total[0:2, :]
    rg_all = rg_total[0:2, :]
    for q in range(16):
        tail_out[152 + 2 * q : 154 + 2 * q, :] = og_all[:, 128 * q : 128 * q + 128] * share
    for q in range(4):
        tail_out[184 + 2 * q : 186 + 2 * q, :] = rg_all[:, 128 * q : 128 * q + 128] * share
    tail_out[192:194, :] = totals[:, :128] * share


def plane_pieces(near, far):
    return near.at[0], far.at[0], near.at[1], far.at[1]


def send_tiles(tiles, buffer, semaphores):
    copies = []
    for k, (fill, target) in enumerate(tiles):
        fill(buffer.at[k])
        copies.append(pltpu.make_async_copy(buffer.at[k], target, semaphores.at[k]))
        copies[-1].start()
    return copies


def finish_middle(info, near, far, near2, far2, *rest):
    out, token, buffer, semaphores = rest[-4:]
    token[...] = jnp.zeros(token.shape, F32)
    tiles = []
    for one, two, bit, partner in (
        (near, far, info[0], False), (near2, far2, 1 - info[0], True)
    ):
        row = pl.ds(pl.multiple_of(256 * bit, 128), 256)
        for piece, block in zip(plane_pieces(one, two), block_order(info, partner)):

            def fill(target, piece=piece):
                for tap in range(9):
                    target[tap] = piece[256 * tap : 256 * tap + 256, :].astype(F32)

            tiles.append((fill, out.at[:, row, lanes(128 * block, 128)]))
    for copy in send_tiles(tiles, buffer, semaphores):
        copy.wait()


def start_outer(
    first, info, mine, pair, expand_out, reduce_out,
    expand_buffer, reduce_buffer, expand_semaphores, reduce_semaphores,
):
    expand_tiles, reduce_tiles = [], []
    for pieces, bit, partner in ((mine, info[0], False), (pair, 1 - info[0], True)):
        order = block_order(info, partner)
        expand_row = pl.ds(pl.multiple_of(256 * bit, 128), 256)
        reduce_row = pl.ds(pl.multiple_of(1024 * bit, 128), 1024)
        for k, block in enumerate((order[1], order[3]) if first else (order[0], order[2])):

            def fill_expand(target, piece=pieces.at[k]):
                for q in range(4):
                    tile = piece[256 * q : 256 * q + 256, :].astype(F32)
                    target[:, 128 * q : 128 * q + 128] = tile

            def fill_reduce(target, piece=pieces.at[k]):
                target[...] = piece[1024:2048, :].astype(F32)

            expand_tiles.append((fill_expand, expand_out.at[expand_row, lanes(512 * block, 512)]))
            reduce_tiles.append((fill_reduce, reduce_out.at[reduce_row, lanes(128 * block, 128)]))
    copies = send_tiles(expand_tiles, expand_buffer, expand_semaphores)
    return copies + send_tiles(reduce_tiles, reduce_buffer, reduce_semaphores)


def finish_outer(first, info, mine, pair, *rest):
    expand_out, reduce_out, token = rest[-7:-4]
    token[...] = jnp.zeros(token.shape, F32)
    for copy in start_outer(first, info, mine, pair, expand_out, reduce_out, *rest[-4:]):
        copy.wait()


def finish_small(
    info, near, far, near2, far2, tail0, tail1, tail2, tail3,
    dsqueeze, dexcite, dfine, dcoarse, stem_out, diff_out, gain_s, bias_s, gain_r, bias_r,
    gain_x, bias_x, scratch, tail,
):
    for one, two, partner in ((near, far, False), (near2, far2, True)):
        for piece, block in zip(plane_pieces(one, two), block_order(info, partner)):
            rows = pl.ds(pl.multiple_of(64 * block, 64), 64)
            here = jnp.concatenate([piece[0:64, :], piece[64:128, :]], 1).astype(F32)
            scratch[rows, :] = scratch[rows, :] + here if partner else here
    tail[...] = tail0[...] + tail1[...] + tail2[...] + tail3[...]
    rows = scratch[...]
    dsqueeze[:, :256] = rows[0:32]
    dsqueeze[:, 256:] = rows[32:64]
    dexcite[:, :256] = rows[64:96]
    dexcite[:, 256:] = rows[96:128]
    for k in range(8):
        dfine[k] = rows[128:160, 32 * k : 32 * k + 32]
    dfine[8] = rows[160:192, 0:32]
    for k in range(9):
        dcoarse[k] = (
            rows[160:192, 32 * (k - 2) : 32 * (k - 2) + 32]
            if 3 <= k < 6
            else jnp.zeros((32, 32), F32)
        )
    stem_out[...] = tail[0:152, :].T[0:64, 0:147]
    for k in range(9):
        diff_out[k] = tail[6 * k : 6 * k + 6, 64:128]
    for q in range(16):
        bias_x[:, 128 * q : 128 * q + 128] = tail[152 + 2 * q : 153 + 2 * q, :]
        gain_x[:, 128 * q : 128 * q + 128] = tail[153 + 2 * q : 154 + 2 * q, :]
    for q in range(4):
        bias_r[:, 128 * q : 128 * q + 128] = tail[184 + 2 * q : 185 + 2 * q, :]
        gain_r[:, 128 * q : 128 * q + 128] = tail[185 + 2 * q : 186 + 2 * q, :]
    bias_s[...] = tail[192:193, :64]
    gain_s[...] = tail[193:194, :64]


def finish_rest(info, near, far, near2, far2, tail0, tail1, tail2, tail3, frames, *rest):
    rest[1][0] = frames[...]
    finish_small(info, near, far, near2, far2, tail0, tail1, tail2, tail3, *rest[2:])


def shape(dims, dtype=F32):
    return jax.ShapeDtypeStruct(dims, dtype)


def whole(dims):
    count = len(dims)
    return pl.BlockSpec(dims, lambda i, *scalars: (0,) * count)


class Far:
    def __init__(self, array, start=0, rows=None, clip=False, split=False, other=None):
        self.array, self.start, self.rows, self.clip = array, start, rows, clip
        self.split, self.other = split, other

    def copies(self):
        return self.array.shape[0] if self.split else 1

    def arrays(self):
        return [self.array] if self.other is None else [self.array, self.other]

    def buffer(self):
        dims = self.array.shape
        if self.clip:
            dims = dims[1:]
        elif self.rows is not None:
            dims = (self.rows,) + dims[1:]
        return pltpu.VMEM(dims, self.array.dtype)

    def source(self, ref, scalars):
        if self.clip:
            return ref.at[scalars[0][0]]
        if self.rows is not None:
            return ref.at[pl.ds(self.start, self.rows)]
        return ref


jax.tree_util.register_pytree_node(
    Far,
    lambda far: ((far.array, far.other), (far.start, far.rows, far.clip, far.split)),
    lambda rest, children: Far(children[0], *rest, children[1]),
)


class FarRef:
    def __init__(self, sources, buffer, semaphores, info):
        self.buffer, self.shape = buffer, buffer.shape
        source = sources[0]
        if len(semaphores) == 1:
            self.copies = [pltpu.make_async_copy(source, buffer, semaphores[0])]
        else:
            self.copies = [
                pltpu.make_async_copy(source.at[k], buffer.at[k], semaphore)
                for k, semaphore in enumerate(semaphores)
            ]
        if len(sources) == 1:
            for copy in self.copies:
                copy.start()
        else:
            other = pltpu.make_async_copy(sources[1], buffer, semaphores[0])
            pl.when(info[info.shape[0] - 1] == 1)(self.copies[0].start)
            pl.when(info[info.shape[0] - 1] == 0)(other.start)
        self.pending = set(range(len(self.copies)))

    def wait(self, part=None):
        for k in sorted(self.pending if part is None else self.pending & {part}):
            self.copies[k].wait()
            self.pending.discard(k)

    def __getitem__(self, place):
        self.wait(place if len(self.copies) > 1 and isinstance(place, int) else None)
        return self.buffer[place]


class FarOut:
    def __init__(self, out, parts=None):
        self.out = out
        self.parts = parts or [(0, out.shape[0])]


class FarOutRef:
    def __init__(self, buffer, home, semaphores, parts):
        self.buffer, self.shape = buffer, buffer.shape
        self.copies = [
            pltpu.make_async_copy(
                buffer.at[pl.ds(start, rows)], home.at[pl.ds(start, rows)], semaphore
            )
            for (start, rows), semaphore in zip(parts, semaphores)
        ]
        self.started = 0

    def __getitem__(self, place):
        return self.buffer[place]

    def __setitem__(self, place, value):
        self.buffer[place] = value

    def flush(self):
        self.copies[self.started].start()
        self.started += 1

    def finish(self):
        while self.started < len(self.copies):
            self.flush()
        for copy in self.copies:
            copy.wait()


def run(
    kernel, outs, arrays, scalars=(), scratch=(), choose=None, deps=(), cost=COST
):
    flat, tree = jax.tree.flatten(tuple(arrays), is_leaf=lambda x: isinstance(x, Far))
    operands, in_specs, places = [], [], []
    for array in flat:
        places.append(len(operands))
        if isinstance(array, Far):
            for piece in array.arrays():
                operands.append(pltpu.with_memory_space_constraint(piece, pltpu.HBM))
                in_specs.append(pl.BlockSpec(memory_space=pltpu.HBM))
            continue
        operands.append(array)
        in_specs.append(whole(array.shape))
    read = len(operands)
    for array in deps:
        operands.append(array)
        in_specs.append(pl.BlockSpec(memory_space=pl.ANY))
    out_specs, out_shape = [], []
    for out in outs:
        if isinstance(out, FarOut):
            out_specs.append(pl.BlockSpec(memory_space=pltpu.HBM))
            out_shape.append(pltpu.HBM(out.out.shape, out.out.dtype))
        else:
            out_specs.append(whole(out.shape))
            out_shape.append(out)
    far_in = [p for p, array in enumerate(flat) if isinstance(array, Far)]
    far_out = [p for p, out in enumerate(outs) if isinstance(out, FarOut)]
    buffers = [flat[p].buffer() for p in far_in]
    buffers += [pltpu.VMEM(outs[p].out.shape, outs[p].out.dtype) for p in far_out]
    moves = len(buffers)
    semaphore_count = sum(flat[p].copies() for p in far_in)
    semaphore_count += sum(len(outs[p].parts) for p in far_out)
    prefetched = tuple(scalars) if choose is None else tuple(scalars) + (choose,)

    def regrouped(*refs):
        first = len(prefetched)
        last = first + len(operands)
        end = last + len(outs)
        near, results = refs[first : first + read], list(refs[last:end])
        kept = refs[end : end + moves]
        semaphores = refs[end + moves] if moves else None
        rest = refs[end + moves + 1 :] if moves else refs[end:]
        ins = [near[place] for place in places]
        used = 0
        for k, p in enumerate(far_in):
            far = flat[p]
            own = [semaphores.at[used + n] for n in range(far.copies())]
            used += far.copies()
            sources = [
                far.source(near[places[p] + j], refs[:first]) for j in range(len(far.arrays()))
            ]
            ins[p] = FarRef(sources, kept[k], own, refs[first - 1])
        for k, p in enumerate(far_out):
            parts = outs[p].parts
            own = [semaphores.at[used + n] for n in range(len(parts))]
            used += len(parts)
            results[p] = FarOutRef(kept[len(far_in) + k], results[p], own, parts)
        kernel(*refs[: len(scalars)], *jax.tree.unflatten(tree, ins), *results, *rest)
        for p in far_in:
            ins[p].wait()
        for p in far_out:
            results[p].finish()

    return pl.pallas_call(
        regrouped,
        grid_spec=pltpu.PrefetchScalarGridSpec(
            num_scalar_prefetch=len(prefetched),
            grid=(1,),
            in_specs=in_specs,
            out_specs=out_specs,
            scratch_shapes=buffers
            + ([pltpu.SemaphoreType.DMA((semaphore_count,))] if moves else [])
            + list(scratch),
        ),
        out_shape=out_shape,
        compiler_params=pltpu.CompilerParams(vmem_limit_bytes=VMEM_BYTES),
        cost_estimate=pl.CostEstimate(flops=cost, bytes_accessed=cost, transcendentals=0),
    )(*prefetched, *operands)


ALL = ("z", "y", "x", "c")


def exchange(value, partner, whole_route=False):
    count = lax.axis_size(ALL)
    route = [(i, partner(i)) for i in range(count) if whole_route or partner(i) != i]
    return lax.ppermute(value, ALL, route)


def by_mask(value, mask):
    return exchange(value, lambda i: i ^ mask)


def bit_count(n):
    count = n.bit_length() - 1
    assert n == 1 << count
    return count


def swap_bits(i, first, second):
    if (i >> first & 1) != (i >> second & 1):
        i ^= (1 << first) | (1 << second)
    return i


def finish(kernel, info, pieces, outs, scratch, into=(), deps=()):
    far = [pl.BlockSpec(memory_space=pltpu.HBM)]
    first = 1 + len(pieces) + len(deps)
    return pl.pallas_call(
        kernel,
        grid_spec=pltpu.PrefetchScalarGridSpec(
            num_scalar_prefetch=1,
            grid=(1,),
            in_specs=[whole(piece.shape) for piece in pieces]
            + [pl.BlockSpec(memory_space=pl.ANY)] * len(deps)
            + far * len(into),
            out_specs=far * len(outs) + [whole((8, 128))],
            scratch_shapes=scratch,
        ),
        out_shape=[pltpu.HBM(out.shape, out.dtype) for out in outs] + [shape((8, 128))],
        input_output_aliases={first + k: k for k in range(len(into))},
        compiler_params=pltpu.CompilerParams(vmem_limit_bytes=VMEM_BYTES),
    )(info, *pieces, *deps, *(pltpu.with_memory_space_constraint(a, pltpu.HBM) for a in into))


def body(
    frames,
    cut_mask,
    offsets,
    stem_kernel,
    diff_kernel,
    stem_gain,
    stem_bias,
    reduce_weight,
    reduce_gain,
    reduce_bias,
    squeeze_weight,
    fine_kernel,
    coarse_kernel,
    excite_weight,
    middle_kernel,
    expand_weight,
    expand_gain,
    expand_bias,
    cotangent,
):
    depth = lax.axis_size("z")
    groups = 2 * depth
    assert frames.shape[0] == MICRO
    bits = bit_count(depth) + 3
    index = lax.axis_index(ALL)
    stem_total = float(4096 * groups)
    row_total = float(128 * groups)
    clip = lax.rem(index, 4).astype(jnp.int32)
    place = clip.reshape(1)
    bit_list = [lax.rem(lax.div(index, 1 << b), 2) for b in range(bits)]
    stays = jnp.where(bit_list[0] == bit_list[2], 1, 0)
    info = jnp.stack(bit_list + [stays]).astype(jnp.int32)
    plane = [(1, 2), (2, 1)]
    plane_mask = 6
    fine_flat = fine_kernel.reshape(288, 32)
    coarse_flat = coarse_kernel.reshape(288, 32)
    gain_s = jnp.tile(stem_gain, 8)[None]
    bias_s = jnp.tile(stem_bias, 8)[None]
    gain_r = reduce_gain[None]
    bias_r = reduce_bias[None]
    gain_x = expand_gain[None]
    bias_x = expand_bias[None]

    def swapped(value, whole_route=False):
        return exchange(value, lambda i: swap_bits(i, 0, 2), whole_route)

    def along(value, choice):
        return exchange(value, lambda i: i ^ (1 << choice[i & 1]))

    def pooled_sum(value):
        return depth_pieces(value + by_mask(value, 1))

    def depth_pieces(value):
        if depth > 4:
            return (lax.psum(value, "z"),)
        return (value,) + tuple(by_mask(value, m << 3) for m in reversed(range(1, depth)))

    def sums_shape(width):
        return shape((2, width))

    def to_plane(pieces):
        own, first, second, both = pieces
        both = by_mask(both, plane_mask)
        return own, along(first, plane[0]), along(second, plane[1]), both

    def padded(rows):
        unit = 16 * depth
        return -(-rows // unit) * unit

    def far(*arrays):
        return tuple(Far(array) for array in arrays)

    def stack(*pieces, deps=()):
        rows = sum(piece.shape[0] for piece in pieces)
        return run(stack_rows, [shape((rows, pieces[0].shape[1]), BF)], pieces, deps=deps)[0]

    def add(first, second, deps=()):
        return run(add_floats, [shape(first.shape)], (first, second), deps=deps)[0]

    def halves(kernel, rows, arrays, deps=()):
        return run(
            kernel, [shape((rows // 2, 128), BF)] * 2, arrays, (info,),
            [pltpu.VMEM((rows, 128), BF)], deps=deps,
        )

    (pack,) = run(
        pack_clip,
        [shape((208, 64), BF)],
        (*far(cut_mask, offsets[None]), Far(frames, clip=True)),
        (place,),
    )
    pack = (pack, swapped(pack))

    def far_pack():
        return Far(pack[0], other=pack[1])

    stem_scratch = [
        pltpu.VMEM((512, 896), BF),
        pltpu.VMEM((256, 384), BF),
        pltpu.VMEM((896, 512), BF),
        pltpu.VMEM((384, 512), BF),
        pltpu.VMEM((192, 128), F32),
        pltpu.VMEM((512, 384), F32),
    ]
    stem_weights = far(stem_kernel.T, diff_kernel)
    v, stem_sums = run(
        stem_front,
        [shape((512, 512)), sums_shape(512)],
        (pack, *stem_weights),
        (info,),
        stem_scratch,
    )
    stem_sums = pooled_sum(stem_sums)
    (cot,) = run(
        lambda place, *refs: copy_rows(*refs),
        [FarOut(shape(cotangent.shape[1:], BF))],
        (Far(cotangent, clip=True),),
        (place,),
        deps=(stem_sums[0],),
    )
    cot_got = swapped(cot)
    stem_norm = far(gain_s, bias_s)
    wide, wide_keep, send, red, red_sums, stem_saved = run(
        functools.partial(stem_close, stem_total),
        [
            FarOut(shape((128, 2048), BF)),
            shape((128, 1024), BF),
            shape((128, 1024), BF),
            shape((128, 512)),
            sums_shape(512),
            FarOut(shape((520, 512))),
        ],
        (v, stem_sums, *stem_norm, Far(reduce_weight)),
        (info,),
    )
    wide_pair = by_mask(send, 1)
    red_sums = pooled_sum(red_sums)
    wide_chip = stack(wide_keep, wide_pair, deps=(red_sums[0], cot_got))
    wide_got = along(wide_chip, plane[0])
    gate_weights = far(squeeze_weight.T, fine_flat, coarse_flat, excite_weight)
    gate_weights += (Far(middle_kernel, split=True),)
    both_keep, send, expanded, exp_sums, saved = run(
        functools.partial(gate_front, row_total),
        [
            shape((128, 512), BF),
            shape((128, 512), BF),
            shape((128, 2048)),
            sums_shape(2048),
            FarOut(shape((264, 512)), [(0, 136), (136, 128)]),
        ],
        (
            red, red_sums, far_pack(), *far(gain_r, bias_r), *gate_weights, Far(expand_weight),
        ),
        (info,),
        [pltpu.VMEM((128, 1024), BF)],
        choose=info,
        deps=(wide_chip,),
    )
    both_pair = by_mask(send, 1)
    exp_sums = pooled_sum(exp_sums)
    both_chip = stack(both_keep, both_pair, deps=(exp_sums[0],))
    both_got = along(both_chip, plane[0])
    wide_near = stack(wide_chip, wide_got, deps=(both_chip,))
    wide_far = along(wide_near, plane[1])
    og_sums, out_saved = run(
        functools.partial(out_back, row_total),
        [
            sums_shape(2048),
            FarOut(shape((264, 2048)), [(0, 64), (128, 64), (64, 64), (192, 72)]),
        ],
        (expanded, exp_sums, *far(gain_x, bias_x, wide), Far(cot, other=cot_got)),
        choose=info,
        deps=(wide_near,),
    )
    og_sums = pooled_sum(og_sums)
    both_near = stack(both_chip, both_got, deps=(og_sums[0],))
    both_far = along(both_near, plane[1])
    hg, og_total, *blocks = run(
        functools.partial(expand_back, row_total),
        [shape((128, 512), BF), FarOut(shape((8, 2048)))] + [shape((128, 640), BF)] * 4,
        (og_sums, Far(out_saved), Far(saved, 136, 128), *far(gain_x, expand_weight)),
        (info,),
        [pltpu.VMEM((128, 512), BF), pltpu.VMEM((128, 2048), BF)],
        deps=(both_near,),
    )
    blocks = to_plane(blocks)
    rg, rg_sums, small = run(
        gate_back,
        [shape((128, 512)), sums_shape(512), shape((256, 256))],
        (far_pack(), hg, Far(saved, 0, 128), *far(gain_r, bias_r), *gate_weights),
        choose=info,
        deps=(wide_far, both_far),
    )
    rg_sums = pooled_sum(rg_sums)
    blocks = stack(*blocks, deps=(rg_sums[0],))
    blocks_pair = by_mask(blocks, 1)

    middle_rows = padded(2304)
    outer_rows = padded(2176)
    depth_bits = list(range(3, bits))
    have = {}
    held = [tuple(rg_sums[1:])]

    def waits():
        deps, held[0] = held[0], ()
        return deps

    def paired(value, rows):
        return value.reshape(2, rows, 128), by_mask(value, 1).reshape(2, rows, 128)

    def halve(name):
        deps = waits()
        for bit in depth_bits[1:]:
            keep, got = have[name]
            keep, send = halves(
                functools.partial(add_halves, bit), keep.shape[0], (keep, got), deps
            )
            have[name] = keep, by_mask(send, 1 << bit)
            deps = ()
        return keep

    def sum_up(name):
        keep, got = have[name]
        (value,) = run(add_rows, [shape(keep.shape, BF)], (keep, got), deps=waits())
        have[name] = value, by_mask(value, 1 << depth_bits[-1])
        return value

    def join(name, depth_range):
        deps = waits()
        for bit in depth_range:
            value, got = have[name]
            rows, width = value.shape
            (value,) = run(
                functools.partial(join_halves, bit),
                [shape((2 * rows, width), BF)],
                (value, got),
                (info,),
                deps=deps,
            )
            if bit > 3:
                have[name] = value, by_mask(value, 1 << (bit - 1))
            deps = ()
        if depth_range[-1] == 3:
            have[name] = value, along(value, plane[1])
        return value

    def near(name, rows):
        value = stack(*have[name], deps=waits())
        have[name + " far"] = along(value, plane[0])
        have[name + " near"] = paired(value, rows)
        return value

    def middle_kernel_sum():
        keep, send = halves(
            middle_weights, middle_rows, ((both_near, both_far), (blocks, blocks_pair)), waits()
        )
        have["middle"] = keep, by_mask(send, 8)
        return keep

    def reduction_back():
        rs, rs_sums, rg_total, *late = run(
            functools.partial(reduce_back, row_total),
            [shape((512, 512)), sums_shape(512), FarOut(shape((8, 512)))]
            + [shape((128, 256), BF)] * 4,
            (
                small, rg, rg_sums, Far(saved, 0, 136), Far(gain_r), Far(out_saved, 0, 128),
                *far(reduce_weight, stem_saved), *stem_norm,
            ),
            (info,),
            [pltpu.VMEM((128, 512), BF)],
            deps=waits(),
        )
        have["rs"] = rs, rs_sums, rg_total
        have["late"] = to_plane(late)
        return rs

    def stem_sum():
        rs_sums = have["rs"][1]
        have["rs here"] = add(rs_sums, by_mask(rs_sums, 1), waits())
        return have["rs here"]

    def late_rows():
        have["late"] = stack(*have["late"], deps=waits())
        have["late pair"] = by_mask(have["late"], 1)
        return have["late"]

    def outer_kernel_sum():
        keep, send = halves(
            outer_weights,
            outer_rows,
            (
                (both_near, both_far), (blocks, blocks_pair), (wide_near, wide_far),
                (have["late"], have["late pair"]),
            ),
            waits(),
        )
        have["outer"] = keep, by_mask(send, 8)
        return keep

    def stem_pieces():
        have["rs pieces"] = depth_pieces(have["rs here"])
        return held[0] + have["rs pieces"]

    def stem_gradient():
        rs, _, rg_total = have["rs"]
        have["frame"], have["tail"] = run(
            functools.partial(stem_back, stem_total, 1.0 / groups),
            [shape((8, 3, 8, 64)), shape((200, 128))],
            (
                far_pack(), *stem_weights, Far(stem_saved), stem_norm[0], rs, have["rs pieces"],
                Far(og_total), Far(rg_total),
            ),
            scratch=stem_scratch,
            choose=info,
            deps=waits(),
        )
        return have["tail"]

    def tail_add(bits_here):
        deps = waits()
        for bit in bits_here:
            have["tail"] = add(have["tail"], by_mask(have["tail"], 1 << bit), deps)
            deps = ()
        return have["tail"]

    def middle_far_rows():
        value = stack(have["middle far"], deps=waits())
        have["middle far"] = paired(value, middle_rows)
        return value

    outer_scratch = [
        pltpu.VMEM((4, 256, 512), F32),
        pltpu.VMEM((4, 1024, 128), F32),
        pltpu.SemaphoreType.DMA((4,)),
        pltpu.SemaphoreType.DMA((4,)),
    ]

    def middle_finish():
        one, two = have["middle near"], have["middle far"]
        have["dmiddle"], token = finish(
            finish_middle,
            info,
            (one[0], two[0], one[1], two[1]),
            [shape((9, 512, 512))],
            [pltpu.VMEM((8, 9, 256, 128), F32), pltpu.SemaphoreType.DMA((8,))],
            deps=waits(),
        )
        return token

    def outer_finish():
        dexpand, dreduce, token = finish(
            functools.partial(finish_outer, False),
            info,
            have["outer near"],
            [shape((512, 2048)), shape((2048, 512))],
            outer_scratch,
            deps=waits(),
        )
        have["outer out"] = dexpand, dreduce
        return token

    steps = {
        "K": middle_kernel_sum,
        "R": reduction_back,
        "Ma": lambda: halve("middle"),
        "Mb": lambda: sum_up("middle"),
        "Mc": lambda: join("middle", depth_bits[:0:-1]),
        "Md": lambda: join("middle", depth_bits[:1]),
        "Mn": lambda: near("middle", middle_rows),
        "Mf": middle_far_rows,
        "Rs": stem_sum,
        "St": late_rows,
        "O": outer_kernel_sum,
        "Oa": lambda: halve("outer"),
        "Ob": lambda: sum_up("outer"),
        "Oc": lambda: join("outer", depth_bits[:0:-1]),
        "Od": lambda: join("outer", depth_bits[:1]),
        "On": lambda: near("outer", outer_rows),
        "Z": stem_pieces,
        "B": stem_gradient,
        "T0": lambda: tail_add([0]),
        "T3": lambda: tail_add(depth_bits[:-1]),
        "T4": lambda: tail_add(depth_bits[-1:]),
        "F": middle_finish,
        "G": outer_finish,
    }
    for name in ORDER:
        result = steps[name]()
        held[0] = result if isinstance(result, tuple) else (result,)
    frame_grad, tail = have["frame"], have["tail"]
    dmiddle = have["dmiddle"]
    dexpand, dreduce = have["outer out"]
    outer_near = have["outer near"]
    token = held[0][0]
    outer_far = have["outer far"]
    frame_grad = swapped(frame_grad, True)
    outer_far = stack(outer_far, deps=(token,))
    outer_far = paired(outer_far, outer_rows)
    tail = (tail,) + tuple(by_mask(tail, mask) for mask in (6, 4, 2))
    dexpand, dreduce, token = finish(
        functools.partial(finish_outer, True),
        info,
        outer_far,
        [shape((512, 2048)), shape((2048, 512))],
        outer_scratch,
        (dexpand, dreduce),
    )
    outer = (outer_near[0], outer_far[0], outer_near[1], outer_far[1])
    small_shapes = ((1, 8, 3, 8, 64), (32, 512), (32, 512), (9, 32, 32), (9, 32, 32), (64, 147))
    small_shapes += ((9, 6, 64),) + tuple((1, n) for n in (64, 64, 512, 512, 2048, 2048))
    (
        frame_grad, dsqueeze, dexcite, dfine, dcoarse, dstem, ddiff, gain_s, bias_s, gain_r,
        bias_r, gain_x, bias_x,
    ) = pl.pallas_call(
        finish_rest,
        grid_spec=pltpu.PrefetchScalarGridSpec(
            num_scalar_prefetch=1,
            grid=(1,),
            in_specs=[pl.BlockSpec((2, 128, 128), lambda i, info: (0, 16, 0))] * 4
            + [whole((200, 128))] * 4
            + [whole((8, 3, 8, 64)), pl.BlockSpec(memory_space=pl.ANY)],
            out_specs=[whole(d) for d in small_shapes],
            scratch_shapes=[pltpu.VMEM((256, 256), F32), pltpu.VMEM((200, 128), F32)],
        ),
        out_shape=[shape(d) for d in small_shapes],
        compiler_params=pltpu.CompilerParams(vmem_limit_bytes=FINISH_BYTES),
    )(info, *outer, *tail, frame_grad, token)
    return (
        frame_grad,
        dstem.T,
        ddiff,
        gain_s[0],
        bias_s[0],
        dreduce,
        gain_r[0],
        bias_r[0],
        dsqueeze.T,
        dfine,
        dcoarse,
        dexcite,
        dmiddle,
        dexpand,
        gain_x[0],
        bias_x[0],
    )


def solution(mesh):
    split = jax.sharding.Mesh(mesh.devices.reshape(-1, 2, 2, 2), ALL)
    copied = P()
    by_group = P(("z", "y"))
    in_specs = (by_group,) * 3 + (copied,) * 15 + (by_group,)
    out_specs = (P(ALL),) + (copied,) * 15
    return jax.shard_map(body, mesh=split, in_specs=in_specs, out_specs=out_specs, check_vma=False)
```

profile of v0, /device:TPU:1, one launch (start us, length us, event | category | flops | bytes accessed | tf_op | source)
XLA Modules:
  0.0 189.9 jit_solution(6946717524736613875)
XLA Ops:
  1.6 4.5 %collective-permute-start = (bf16[208,64]{1,0:T(8,128)(2,1)S(1)}, bf16[208,64]{1,0:T(8,128)(2,1)S(1)}, u32[]{:S(2)}, u32[]{:S(2)}) collective-permute-start(bf16[208,64]{1,0:T(8,128)(2,1)S(1)} %shard_map.306.refs_1_.refs_7_), channel_id=1, source_target_pairs={{1,4},{3,6},{4,1},{6,3},{9,12},{11,14},{12,9},{14,11},{17,20},{19,... | collective-permute-start | bytes 79880 | tf_op jit(solution)/shard_map/ppermute | solution.py:942
  7.9 2.8 %shard_map.307 = (f32[512,512]{1,0:T(8,128)S(1)}, f32[2,512]{1,0:T(2,128)S(1)}) custom-call(s32[6]{0:T(128)S(1)} %stack.27.refs_0_.refs_1_.info, bf16[208,64]{1,0:T(8,128)(2,1)S(1)} %shard_map.306.refs_1_.refs_7_, bf16[208,64]{1,0:T(8,128)(2,1)S(1)} %collective-permute-done.refs_2_.refs_8_, bf16[64,147]{1,0:T(8,128)(2,1)} %bitcast.50, bf16[9,6,64]{2,1,0:T(8,128)(2,1)} %refs_4_.3), custom_call_target="tpu_custom_call" | custom-call | flops 1000000 | bytes 1000000 | tf_op jit(solution)/shard_map/pallas_call | solution.py:919
  14.0 3.6 %collective-permute-start.10 = (bf16[8,2,8,2048]{3,2,1,0:T(8,128)(2,1)}, bf16[8,2,8,2048]{3,2,1,0:T(8,128)(2,1)S(1)}, u32[]{:S(2)}, u32[]{:S(2)}) collective-permute-start(bf16[8,2,8,2048]{3,2,1,0:T(8,128)(2,1)} %shard_map.309.refs_9_), channel_id=1, source_target_pairs={{1,4},{3,6},{4,1},{6,3},{9,12},{11,14},{12,9},{14,11},{17,20},{19,... | collective-permute-start | bytes 1572872 | tf_op jit(solution)/shard_map/ppermute | solution.py:942
  17.6 3.4 %collective-permute-start.2 = (f32[2,512]{1,0:T(2,128)S(1)}, f32[2,512]{1,0:T(2,128)S(1)}, u32[]{:S(2)}, u32[]{:S(2)}) collective-permute-start(f32[2,512]{1,0:T(2,128)S(1)} %add.27.refs_2_), channel_id=1, source_target_pairs={{0,24},{1,25},{2,26},{3,27},{4,28},{5,29},{6,30},{7,31},{8,16},{9,... | collective-permute-start | bytes 12296 | tf_op jit(solution)/shard_map/ppermute | solution.py:942
  24.4 2.8 %shard_map.308 = (bf16[128,2048]{1,0:T(8,128)(2,1)}, bf16[128,1024]{1,0:T(8,128)(2,1)S(1)}, bf16[128,1024]{1,0:T(8,128)(2,1)S(1)}, f32[128,512]{1,0:T(8,128)S(1)...) custom-call(s32[6]{0:T(128)S(1)} %stack.27.refs_0_.refs_1_.info, f32[512,512]{1,0:T(8,128)S(1)} %get-tuple-element.78.refs_1_, ...), custom_call_target="tpu_custom_call" | custom-call | flops 1000000 | bytes 1000000 | tf_op jit(solution)/shard_map/pallas_call | solution.py:919
  35.0 4.5 %shard_map.311 = (bf16[128,512]{1,0:T(8,128)(2,1)S(1)}, bf16[128,512]{1,0:T(8,128)(2,1)S(1)}, f32[128,2048]{1,0:T(8,128)S(1)}, f32[2,2048]{1,0:T(2,128)S(1)}, f32[264,512]{1,0:T(8,128)}) custom-call(s32[6]{0:T(128)S(1)} %stack.27.refs_0_.refs_1_.info, s32[6]{0:T(128)S(1)} %stack.27.refs_0_.refs_1_.info, f32[128,512]{1,0:T(8,128)S(1)} %get-tuple-element.80.refs_2_, ...), custom_call_target="tpu_custom_call" | custom-call | flops 1000000 | bytes 1000000 | tf_op jit(solution)/shard_map/pallas_call | solution.py:919
  50.1 3.5 %shard_map.314 = (f32[2,2048]{1,0:T(2,128)S(1)}, f32[264,2048]{1,0:T(8,128)}) custom-call(s32[6]{0:T(128)S(1)} %stack.27.refs_0_.refs_1_.info, f32[128,2048]{1,0:T(8,128)S(1)} %get-tuple-element.87.refs_1_, f32[2,2048]{1,0:T(2,128)S(1)} %add.29.refs_2_, f32[2,2048]{1,0:T(2,128)S(1)} %collective-permute-done.14.refs_3_, ...), custom_call_target="tpu_custom_call" | custom-call | flops 1000000 | bytes 1000000 | tf_op jit(solution)/shard_map/pallas_call | solution.py:919
  63.1 3.9 %shard_map.316 = (bf16[128,512]{1,0:T(8,128)(2,1)S(1)}, f32[8,2048]{1,0:T(8,128)}, bf16[128,640]{1,0:T(8,128)(2,1)S(1)}, bf16[128,640]{1,0:T(8,128)(2,1)S(1)}, b...) custom-call(s32[6]{0:T(128)S(1)} %stack.27.refs_0_.refs_1_.info, f32[2,2048]{1,0:T(2,128)S(1)} %add.30.refs_2_.refs_1_, ...), custom_call_target="tpu_custom_call" | custom-call | flops 1000000 | bytes 1000000 | tf_op jit(solution)/shard_map/pallas_call | solution.py:919
  69.7 5.3 %shard_map.317 = (f32[128,512]{1,0:T(8,128)S(1)}, f32[2,512]{1,0:T(2,128)S(1)}, f32[256,256]{1,0:T(8,128)S(1)}) custom-call(s32[6]{0:T(128)S(1)} %stack.27.refs_0_.refs_1_.info, bf16[208,64]{1,0:T(8,128)(2,1)} %copy-done.1, bf16[208,64]{1,0:T(8,128)(2,1)} %copy-done.2, bf16[128,512]{1,0:T(8,128)(2,1)S(1)} %get-tuple-element.96.refs_3_, ...), custom_call_target="tpu_custom_call" | custom-call | flops 1000000 | bytes 1000000 | tf_op jit(solution)/shard_map/pallas_call | solution.py:919
  86.8 4.4 %shard_map.320 = (f32[512,512]{1,0:T(8,128)S(1)}, f32[2,512]{1,0:T(2,128)S(1)}, f32[8,512]{1,0:T(8,128)}, bf16[128,256]{1,0:T(8,128)(2,1)S(1)}, bf16[128,256]{1,...) custom-call(s32[6]{0:T(128)S(1)} %stack.27.refs_0_.refs_1_.info, ...), custom_call_target="tpu_custom_call" | custom-call | flops 1000000 | bytes 1000000 | tf_op jit(solution)/shard_map/pallas_call | solution.py:919
  98.0 2.9 %collective-permute-start.36 = (bf16[512,256]{1,0:T(8,128)(2,1)S(1)}, bf16[512,256]{1,0:T(8,128)(2,1)S(1)}, u32[]{:S(2)}, u32[]{:S(2)}) collective-permute-start(bf16[512,256]{1,0:T(8,128)(2,1)S(1)} %shard_map.322.refs_2_.refs_7_), channel_id=1, source_target_pairs={{0,1},{1,0},{2,3},{3,2},{4,5},{5,4},{6,7},{7,6},{8,9},{9,8},{10,11... | collective-permute-start | bytes 786440 | tf_op jit(solution)/shard_map/ppermute | solution.py:942
  104.6 6.3 %collective-permute-done.40.refs_2_ = bf16[576,128]{1,0:T(8,128)(2,1)S(1)} collective-permute-done((bf16[576,128]{1,0:T(8,128)(2,1)S(1)}, bf16[576,128]{1,0:T(8,128)(2,1)S(1)}, u32[]{:S(2)}, u32[]{:S(2)}) %collective-permute-start.40) | collective-permute-done | bytes 147488 | tf_op jit(solution)/shard_map/ppermute | solution.py:942
  116.5 7.9 %collective-permute-done.39.refs_2_ = bf16[1088,128]{1,0:T(8,128)(2,1)S(1)} collective-permute-done((bf16[1088,128]{1,0:T(8,128)(2,1)S(1)}, bf16[1088,128]{1,0:T(8,128)(2,1)S(1)}, u32[]{:S(2)}, u32[]{:S(2)}) %collective-permute-start.39) | collective-permute-done | bytes 278560 | tf_op jit(solution)/shard_map/ppermute | solution.py:942
  127.4 7.1 %shard_map.329 = (f32[8,3,8,64]{3,2,1,0:T(8,128)S(1)}, f32[200,128]{1,0:T(8,128)S(1)}) custom-call(s32[6]{0:T(128)S(1)} %stack.27.refs_0_.refs_1_.info, bf16[208,64]{1,0:T(8,128)(2,1)} %copy-done.1, bf16[208,64]{1,0:T(8,128)(2,1)} %copy-done.2, bf16[64,147]{1,0:T(8,128)(2,1)} %bitcast.51, bf16[9,6,64]{2,1,0:T(8,128)(2,1)} %refs_4_.3, ...), custom_call_target="tpu_custom_call" | custom-call | flops 1000000 | bytes 1000000 | tf_op jit(solution)/shard_map/pallas_call | solution.py:919
  137.3 5.1 %collective-permute-done.46.refs_2_ = bf16[544,128]{1,0:T(8,128)(2,1)S(1)} collective-permute-done((bf16[544,128]{1,0:T(8,128)(2,1)S(1)}, bf16[544,128]{1,0:T(8,128)(2,1)S(1)}, u32[]{:S(2)}, u32[]{:S(2)}) %collective-permute-start.46) | collective-permute-done | bytes 139296 | tf_op jit(solution)/shard_map/ppermute | solution.py:942
  143.1 5.7 %collective-permute-done.48.refs_2_ = bf16[1088,128]{1,0:T(8,128)(2,1)S(1)} collective-permute-done((bf16[1088,128]{1,0:T(8,128)(2,1)S(1)}, bf16[1088,128]{1,0:T(8,128)(2,1)S(1)}, u32[]{:S(2)}, u32[]{:S(2)}) %collective-permute-start.48) | collective-permute-done | bytes 278560 | tf_op jit(solution)/shard_map/ppermute | solution.py:942
  150.9 4.1 %collective-permute-start.50 = (f32[200,128]{1,0:T(8,128)S(1)}, f32[200,128]{1,0:T(8,128)S(1)}, u32[]{:S(2)}, u32[]{:S(2)}) collective-permute-start(f32[200,128]{1,0:T(8,128)S(1)} %get-tuple-element.117.refs_2_.refs_0_), channel_id=1, source_target_pairs={{0,1},{1,0},{2,3},{3,2},{4,5},{5,4},{6,7},{7,6},{8,9},{9,8},{10,11... | collective-permute-start | bytes 307208 | tf_op jit(solution)/shard_map/ppermute | solution.py:942
  156.9 3.2 %collective-permute-done.51.refs_1_ = f32[200,128]{1,0:T(8,128)S(1)} collective-permute-done((f32[200,128]{1,0:T(8,128)S(1)}, f32[200,128]{1,0:T(8,128)S(1)}, u32[]{:S(2)}, u32[]{:S(2)}) %collective-permute-start.51) | collective-permute-done | bytes 102432 | tf_op jit(solution)/shard_map/ppermute | solution.py:942
  160.4 3.2 %collective-permute-start.54 = (bf16[4352,128]{1,0:T(8,128)(2,1)S(1)}, bf16[4352,128]{1,0:T(8,128)(2,1)S(1)}, u32[]{:S(2)}, u32[]{:S(2)}) collective-permute-start(bf16[4352,128]{1,0:T(8,128)(2,1)S(1)} %shard_map.337.rest_0_), channel_id=1, source_target_pairs={{0,1},{1,0},{2,3},{3,2},{4,5},{5,4},{6,7},{7,6},{8,9},{9,8},{10,11... | collective-permute-start | bytes 3342344 | tf_op jit(solution)/shard_map/ppermute | solution.py:942
  165.2 4.3 %shard_map.338 = (f32[9,512,512]{2,1,0:T(8,128)}, f32[8,128]{1,0:T(8,128)S(1)}) custom-call(s32[6]{0:T(128)S(1)} %stack.27.refs_0_.refs_1_.info, bf16[2,2304,128]{2,1,0:T(8,128)(2,1)S(1)} %bitcast.34, bf16[2,2304,128]{2,1,0:T(8,128)(2,1)S(1)} %bitcast.35, bf16[2,2304,128]{2,1,0:T(8,128)(2,1)S(1)} %bitcast.42, bf16[2,2304,128]{2,1,0:T(8,128)(2,1)S(1)} %bitcast.43, ...), custom_call_target="tpu_custom_call" | custom-call | tf_op jit(solution)/shard_map/pallas_call | solution.py:964
  171.6 2.7 %shard_map.340 = (f32[512,2048]{1,0:T(8,128)}, f32[2048,512]{1,0:T(8,128)}, f32[8,128]{1,0:T(8,128)S(1)}) custom-call(s32[6]{0:T(128)S(1)} %stack.27.refs_0_.refs_1_.info, bf16[2,2176,128]{2,1,0:T(8,128)(2,1)S(1)} %bitcast.32, bf16[2,2176,128]{2,1,0:T(8,128)(2,1)S(1)} %bitcast.38, f32[200,128]{1,0:T(8,128)S(1)} %shard_map.339.rest_0_.tail0), custom_call_target="tpu_custom_call" | custom-call | tf_op jit(solution)/shard_map/pallas_call | solution.py:964
  174.3 3.9 %collective-permute-done.53.refs_0_ = bf16[4352,128]{1,0:T(8,128)(2,1)S(1)} collective-permute-done((bf16[4352,128]{1,0:T(8,128)(2,1)S(1)}, bf16[4352,128]{1,0:T(8,128)(2,1)S(1)}, u32[]{:S(2)}, u32[]{:S(2)}) %collective-permute-start.53) | collective-permute-done | bytes 1114144 | tf_op jit(solution)/shard_map/ppermute | solution.py:942
  182.1 3.3 %collective-permute-start.62 = (f32[8,3,8,64]{3,2,1,0:T(8,128)S(1)}, f32[8,3,8,64]{3,2,1,0:T(8,128)S(1)}, u32[]{:S(2)}, u32[]{:S(2)}) collective-permute-start(f32[8,3,8,64]{3,2,1,0:T(8,128)S(1)} %get-tuple-element.120), channel_id=1, source_target_pairs={{0,0},{1,4},{2,2},{3,6},{4,1},{5,5},{6,3},{7,7},{8,8},{9,12},{10,1... | collective-permute-start | bytes 147464 | tf_op jit(solution)/shard_map/ppermute | solution.py:942
  185.5 2.7 %shard_map.342 = (f32[512,2048]{1,0:T(8,128)}, f32[2048,512]{1,0:T(8,128)}, f32[8,128]{1,0:T(8,128)S(1)}) custom-call(s32[6]{0:T(128)S(1)} %stack.27.refs_0_.refs_1_.info, bf16[2,2176,128]{2,1,0:T(8,128)(2,1)S(1)} %bitcast.36, bf16[2,2176,128]{2,1,0:T(8,128)(2,1)S(1)} %bitcast.40, ...), custom_call_target="tpu_custom_call", output_to_operand_aliasing={{0}: (3, {}), {1}: (4, {})} | custom-call | tf_op jit(solution)/shard_map/pallas_call | solution.py:964
  (160 shorter events, 87.4 us)
Async XLA Ops:
  14.0 14.8 %collective-permute-start.10 = (bf16[8,2,8,2048]{3,2,1,0:T(8,128)(2,1)}, bf16[8,2,8,2048]{3,2,1,0:T(8,128)(2,1)S(1)}, u32[]{:S(2)}, u32[]{:S(2)}) collective-permute-start(bf16[8,2,8,2048]{3,2,1,0:T(8,128)(2,1)} %shard_map.309.refs_9_), channel_id=1, source_target_pairs={{1,4},{3,6},{4,1},{6,3},{9,12},{11,14},{12,9},{14,11},{17,20},{19,... | collective-permute-start | bytes 1572872 | tf_op jit(solution)/shard_map/ppermute | solution.py:942
  28.8 13.8 %collective-permute-start.17 = (bf16[256,1024]{1,0:T(8,128)(2,1)S(1)}, bf16[256,1024]{1,0:T(8,128)(2,1)S(1)}, u32[]{:S(2)}, u32[]{:S(2)}) collective-permute-start(bf16[256,1024]{1,0:T(8,128)(2,1)S(1)} %shard_map.310.refs_17_.refs_0_), channel_id=1, source_target_pairs={{0,2},{1,5},{2,0},{3,7},{4,6},{5,1},{6,4},{7,3},{8,10},{9,13},{10,... | collective-permute-start | bytes 1572872 | tf_op jit(solution)/shard_map/ppermute | solution.py:942
  42.7 27.0 %collective-permute-start.26 = (bf16[512,1024]{1,0:T(8,128)(2,1)S(1)}, bf16[512,1024]{1,0:T(8,128)(2,1)S(1)}, u32[]{:S(2)}, u32[]{:S(2)}) collective-permute-start(bf16[512,1024]{1,0:T(8,128)(2,1)S(1)} %shard_map.313.refs_11_.refs_5_), channel_id=1, source_target_pairs={{0,4},{1,3},{2,6},{3,1},{4,0},{5,7},{6,2},{7,5},{8,12},{9,11},{10,... | collective-permute-start | bytes 3145736 | tf_op jit(solution)/shard_map/ppermute | solution.py:942
  43.1 13.6 %collective-permute-start.13 = (bf16[256,512]{1,0:T(8,128)(2,1)S(1)}, bf16[256,512]{1,0:T(8,128)(2,1)S(1)}, u32[]{:S(2)}, u32[]{:S(2)}) collective-permute-start(bf16[256,512]{1,0:T(8,128)(2,1)S(1)} %shard_map.312.refs_2_.refs_0_), channel_id=1, source_target_pairs={{0,2},{1,5},{2,0},{3,7},{4,6},{5,1},{6,4},{7,3},{8,10},{9,13},{10,... | collective-permute-start | bytes 786440 | tf_op jit(solution)/shard_map/ppermute | solution.py:942
  56.8 13.0 %collective-permute-start.19 = (bf16[512,512]{1,0:T(8,128)(2,1)S(1)}, bf16[512,512]{1,0:T(8,128)(2,1)S(1)}, u32[]{:S(2)}, u32[]{:S(2)}) collective-permute-start(bf16[512,512]{1,0:T(8,128)(2,1)S(1)} %shard_map.315.refs_9_.refs_1_), channel_id=1, source_target_pairs={{0,4},{1,3},{2,6},{3,1},{4,0},{5,7},{6,2},{7,5},{8,12},{9,11},{10,... | collective-permute-start | bytes 1572872 | tf_op jit(solution)/shard_map/ppermute | solution.py:942
  67.0 10.8 %collective-permute-start.23 = (bf16[128,640]{1,0:T(8,128)(2,1)S(1)}, bf16[128,640]{1,0:T(8,128)(2,1)S(1)}, u32[]{:S(2)}, u32[]{:S(2)}) collective-permute-start(bf16[128,640]{1,0:T(8,128)(2,1)S(1)} %get-tuple-element.93), channel_id=1, source_target_pairs={{0,2},{1,5},{2,0},{3,7},{4,6},{5,1},{6,4},{7,3},{8,10},{9,13},{10,... | collective-permute-start | bytes 491528 | tf_op jit(solution)/shard_map/ppermute | solution.py:942
  67.1 10.7 %collective-permute-start.24 = (bf16[128,640]{1,0:T(8,128)(2,1)S(1)}, bf16[128,640]{1,0:T(8,128)(2,1)S(1)}, u32[]{:S(2)}, u32[]{:S(2)}) collective-permute-start(bf16[128,640]{1,0:T(8,128)(2,1)S(1)} %get-tuple-element.94), channel_id=1, source_target_pairs={{0,4},{1,3},{2,6},{3,1},{4,0},{5,7},{6,2},{7,5},{8,12},{9,11},{10,... | collective-permute-start | bytes 491528 | tf_op jit(solution)/shard_map/ppermute | solution.py:942
  67.5 10.3 %collective-permute-start.25 = (bf16[128,640]{1,0:T(8,128)(2,1)S(1)}, bf16[128,640]{1,0:T(8,128)(2,1)S(1)}, u32[]{:S(2)}, u32[]{:S(2)}) collective-permute-start(bf16[128,640]{1,0:T(8,128)(2,1)S(1)} %get-tuple-element.95), channel_id=1, source_target_pairs={{0,6},{1,7},{2,4},{3,5},{4,2},{5,3},{6,0},{7,1},{8,14},{9,15},{10,... | collective-permute-start | bytes 491528 | tf_op jit(solution)/shard_map/ppermute | solution.py:942
  86.1 7.8 %collective-permute-start.35 = (bf16[1152,128]{1,0:T(8,128)(2,1)S(1)}, bf16[1152,128]{1,0:T(8,128)(2,1)S(1)}, u32[]{:S(2)}, u32[]{:S(2)}) collective-permute-start(bf16[1152,128]{1,0:T(8,128)(2,1)S(1)} %get-tuple-element.106), channel_id=1, source_target_pairs={{0,8},{1,9},{2,10},{3,11},{4,12},{5,13},{6,14},{7,15},{8,0},{9,1},... | collective-permute-start | bytes 884744 | tf_op jit(solution)/shard_map/ppermute | solution.py:942
  102.1 8.8 %collective-permute-start.40 = (bf16[576,128]{1,0:T(8,128)(2,1)S(1)}, bf16[576,128]{1,0:T(8,128)(2,1)S(1)}, u32[]{:S(2)}, u32[]{:S(2)}) collective-permute-start(bf16[576,128]{1,0:T(8,128)(2,1)S(1)} %shard_map.324.refs_9_.refs_1_), channel_id=1, source_target_pairs={{0,16},{1,17},{2,18},{3,19},{4,20},{5,21},{6,22},{7,23},{8,24},{9,... | collective-permute-start | bytes 442376 | tf_op jit(solution)/shard_map/ppermute | solution.py:942
  111.5 14.0 %collective-permute-start.45 = (bf16[1152,128]{1,0:T(8,128)(2,1)S(1)}, bf16[1152,128]{1,0:T(8,128)(2,1)S(1)}, u32[]{:S(2)}, u32[]{:S(2)}) collective-permute-start(bf16[1152,128]{1,0:T(8,128)(2,1)S(1)} %shard_map.326.refs_3_.refs_1_), channel_id=1, source_target_pairs={{0,8},{1,9},{2,10},{3,11},{4,12},{5,13},{6,14},{7,15},{8,0},{9,1},... | collective-permute-start | bytes 884744 | tf_op jit(solution)/shard_map/ppermute | solution.py:942
  111.5 12.9 %collective-permute-start.39 = (bf16[1088,128]{1,0:T(8,128)(2,1)S(1)}, bf16[1088,128]{1,0:T(8,128)(2,1)S(1)}, u32[]{:S(2)}, u32[]{:S(2)}) collective-permute-start(bf16[1088,128]{1,0:T(8,128)(2,1)S(1)} %get-tuple-element.112), channel_id=1, source_target_pairs={{0,8},{1,9},{2,10},{3,11},{4,12},{5,13},{6,14},{7,15},{8,0},{9,1},... | collective-permute-start | bytes 835592 | tf_op jit(solution)/shard_map/ppermute | solution.py:942
  113.0 12.4 %collective-permute-start.42 = (f32[2,512]{1,0:T(2,128)S(1)}, f32[2,512]{1,0:T(2,128)S(1)}, u32[]{:S(2)}, u32[]{:S(2)}) collective-permute-start(f32[2,512]{1,0:T(2,128)S(1)} %shard_map.323.refs_2_.refs_4_.refs_8_), channel_id=1, source_target_pairs={{0,24},{1,25},{2,26},{3,27},{4,28},{5,29},{6,30},{7,31},{8,16},{9,... | collective-permute-start | bytes 12296 | tf_op jit(solution)/shard_map/ppermute | solution.py:942
  115.0 10.4 %collective-permute-start.43 = (f32[2,512]{1,0:T(2,128)S(1)}, f32[2,512]{1,0:T(2,128)S(1)}, u32[]{:S(2)}, u32[]{:S(2)}) collective-permute-start(f32[2,512]{1,0:T(2,128)S(1)} %shard_map.323.refs_2_.refs_4_.refs_8_), channel_id=1, source_target_pairs={{0,16},{1,17},{2,18},{3,19},{4,20},{5,21},{6,22},{7,23},{8,24},{9,... | collective-permute-start | bytes 12296 | tf_op jit(solution)/shard_map/ppermute | solution.py:942
  115.1 10.4 %collective-permute-start.44 = (f32[2,512]{1,0:T(2,128)S(1)}, f32[2,512]{1,0:T(2,128)S(1)}, u32[]{:S(2)}, u32[]{:S(2)}) collective-permute-start(f32[2,512]{1,0:T(2,128)S(1)} %shard_map.323.refs_2_.refs_4_.refs_8_), channel_id=1, source_target_pairs={{0,8},{1,9},{2,10},{3,11},{4,12},{5,13},{6,14},{7,15},{8,0},{9,1},... | collective-permute-start | bytes 12296 | tf_op jit(solution)/shard_map/ppermute | solution.py:942
  126.0 9.1 %collective-permute-start.47 = (bf16[2304,128]{1,0:T(8,128)(2,1)S(1)}, bf16[2304,128]{1,0:T(8,128)(2,1)S(1)}, u32[]{:S(2)}, u32[]{:S(2)}) collective-permute-start(bf16[2304,128]{1,0:T(8,128)(2,1)S(1)} %shard_map.328.refs_14_.refs_0_), channel_id=1, source_target_pairs={{0,4},{1,3},{2,6},{3,1},{4,0},{5,7},{6,2},{7,5},{8,12},{9,11},{10,... | collective-permute-start | bytes 1769480 | tf_op jit(solution)/shard_map/ppermute | solution.py:942
  126.1 8.4 %collective-permute-start.41 = (bf16[544,128]{1,0:T(8,128)(2,1)S(1)}, bf16[544,128]{1,0:T(8,128)(2,1)S(1)}, u32[]{:S(2)}, u32[]{:S(2)}) collective-permute-start(bf16[544,128]{1,0:T(8,128)(2,1)S(1)} %get-tuple-element.114), channel_id=1, source_target_pairs={{0,16},{1,17},{2,18},{3,19},{4,20},{5,21},{6,22},{7,23},{8,24},{9,... | collective-permute-start | bytes 417800 | tf_op jit(solution)/shard_map/ppermute | solution.py:942
  135.2 21.3 %collective-permute-start.52 = (bf16[4608,128]{1,0:T(8,128)(2,1)S(1)}, bf16[4608,128]{1,0:T(8,128)(2,1)S(1)}, u32[]{:S(2)}, u32[]{:S(2)}) collective-permute-start(bf16[4608,128]{1,0:T(8,128)(2,1)S(1)} %shard_map.331.refs_3_), channel_id=1, source_target_pairs={{0,2},{1,5},{2,0},{3,7},{4,6},{5,1},{6,4},{7,3},{8,10},{9,13},{10,... | collective-permute-start | bytes 3538952 | tf_op jit(solution)/shard_map/ppermute | solution.py:942
  149.3 10.9 %collective-permute-start.49 = (bf16[2176,128]{1,0:T(8,128)(2,1)S(1)}, bf16[2176,128]{1,0:T(8,128)(2,1)S(1)}, u32[]{:S(2)}, u32[]{:S(2)}) collective-permute-start(bf16[2176,128]{1,0:T(8,128)(2,1)S(1)} %shard_map.333.refs_2_.refs_0_), channel_id=1, source_target_pairs={{0,4},{1,3},{2,6},{3,1},{4,0},{5,7},{6,2},{7,5},{8,12},{9,11},{10,... | collective-permute-start | bytes 1671176 | tf_op jit(solution)/shard_map/ppermute | solution.py:942
  156.0 9.2 %collective-permute-start.56 = (bf16[4608,128]{1,0:T(8,128)(2,1)S(1)}, bf16[4608,128]{1,0:T(8,128)(2,1)S(1)}, u32[]{:S(2)}, u32[]{:S(2)}) collective-permute-start(bf16[4608,128]{1,0:T(8,128)(2,1)S(1)} %shard_map.331.refs_3_), channel_id=1, source_target_pairs={{0,1},{1,0},{2,3},{3,2},{4,5},{5,4},{6,7},{7,6},{8,9},{9,8},{10,11... | collective-permute-start | bytes 3538952 | tf_op jit(solution)/shard_map/ppermute | solution.py:942
  156.5 8.7 %collective-permute-start.57 = (bf16[4608,128]{1,0:T(8,128)(2,1)S(1)}, bf16[4608,128]{1,0:T(8,128)(2,1)S(1)}, u32[]{:S(2)}, u32[]{:S(2)}) collective-permute-start(bf16[4608,128]{1,0:T(8,128)(2,1)S(1)} %shard_map.335.refs_2_), channel_id=1, source_target_pairs={{0,1},{1,0},{2,3},{3,2},{4,5},{5,4},{6,7},{7,6},{8,9},{9,8},{10,11... | collective-permute-start | bytes 3538952 | tf_op jit(solution)/shard_map/ppermute | solution.py:942
  160.4 11.3 %collective-permute-start.54 = (bf16[4352,128]{1,0:T(8,128)(2,1)S(1)}, bf16[4352,128]{1,0:T(8,128)(2,1)S(1)}, u32[]{:S(2)}, u32[]{:S(2)}) collective-permute-start(bf16[4352,128]{1,0:T(8,128)(2,1)S(1)} %shard_map.337.rest_0_), channel_id=1, source_target_pairs={{0,1},{1,0},{2,3},{3,2},{4,5},{5,4},{6,7},{7,6},{8,9},{9,8},{10,11... | collective-permute-start | bytes 3342344 | tf_op jit(solution)/shard_map/ppermute | solution.py:942
  163.6 14.6 %collective-permute-start.53 = (bf16[4352,128]{1,0:T(8,128)(2,1)S(1)}, bf16[4352,128]{1,0:T(8,128)(2,1)S(1)}, u32[]{:S(2)}, u32[]{:S(2)}) collective-permute-start(bf16[4352,128]{1,0:T(8,128)(2,1)S(1)} %shard_map.337.rest_0_), channel_id=1, source_target_pairs={{0,2},{1,5},{2,0},{3,7},{4,6},{5,1},{6,4},{7,3},{8,10},{9,13},{10,... | collective-permute-start | bytes 3342344 | tf_op jit(solution)/shard_map/ppermute | solution.py:942
  179.3 8.8 %collective-permute-start.59 = (f32[200,128]{1,0:T(8,128)S(1)}, f32[200,128]{1,0:T(8,128)S(1)}, u32[]{:S(2)}, u32[]{:S(2)}) collective-permute-start(f32[200,128]{1,0:T(8,128)S(1)} %shard_map.339.rest_0_.tail0), channel_id=1, source_target_pairs={{0,6},{1,7},{2,4},{3,5},{4,2},{5,3},{6,0},{7,1},{8,14},{9,15},{10,... | collective-permute-start | bytes 307208 | tf_op jit(solution)/shard_map/ppermute | solution.py:942
  (44 other events, 212.3 us)
where the time goes:
time: 190 us
  starting transfers between devices  76 us (40%)
  Pallas kernels  56.2 us (30%)
  waiting for transfers between devices  54.9 us (29%)
    ppermute x63, starting transfers between devices, exchange(): return lax.ppermute(value, ALL, route)  76 us
    ppermute x63, waiting for transfers between devices, exchange(): return lax.ppermute(value, ALL, route)  54.9 us
    pallas_call x34, Pallas kernels, run(): pl.pallas_call(regrouped, grid_spec=pltpu.PrefetchScalarGridSpec(num_scal...  45 us
    pallas_call x3, Pallas kernels, finish(): pl.pallas_call(kernel, grid_spec=pltpu.PrefetchScalarGridSpec(num_scalar_...  9.67 us
  transfers between devices with their start and end apart: 63, of which 30 were waited for; matrix products, arithmetic and copies ran while one was open for 1% of the time, Pallas kernels for 24%

commit v1 on v0

--- a/solution.py
+++ b/solution.py
@@ -315,9 +315,10 @@
     column_sums(sums_out, expanded, expanded * expanded)
 
 
-def out_back(row_total, expanded, sums, gain, bias, wide, cot, sums_out, save):
+def out_back(row_total, expanded, sums, gain, bias, wide, cot, sums_out, save, scale_out):
     mean, scale = norm_scale(summed_up(sums), row_total)
-    save[256:257, :] = scale
+    scale_out[0:1, :] = scale
+    scale_out.flush()
     first = jnp.zeros((1, 2048), F32)
     second = jnp.zeros((1, 2048), F32)
     for hb in range(2):
@@ -329,8 +330,8 @@
         y = normal * gain[...] + bias[...] + wide[part, :].astype(F32)
         weightless = cot[:, hb, :, :].astype(F32).reshape(64, 2048)
         og = weightless * swish_slope(y)
-        save[part, :] = og
-        save[128 + 64 * hb : 192 + 64 * hb, :] = normal
+        save[part, :] = og.astype(BF)
+        save[128 + 64 * hb : 192 + 64 * hb, :] = normal.astype(BF)
         first = first + jnp.sum(og, 0, keepdims=True)
         second = second + jnp.sum(og * normal, 0, keepdims=True)
     spread_sums(sums_out, first, second)
@@ -359,14 +360,15 @@
 
 
 def expand_back(
-    row_total, info, grad_sums, saved, hpre, gain, expand, hg_out, total_out, *rest
+    row_total, info, grad_sums, saved, scale, hpre, gain, expand, hg_out, total_out, *rest
 ):
     outs, (hg_scratch, dv_scratch) = rest[:4], rest[4:]
     sums = summed_up(grad_sums)
     total_out[0:2, :] = sums
     total_out.flush()
     dv = norm_pull(
-        saved[0:128, :], saved[128:256, :], saved[256:257, :], gain[...], sums, row_total
+        saved[0:128, :].astype(F32), saved[128:256, :].astype(F32), scale[0:1, :], gain[...],
+        sums, row_total,
     ).astype(BF)
     dv_scratch[...] = dv
     dhid = dot_nt(dv, expand[...]).astype(BF).astype(F32)
@@ -1143,11 +1145,12 @@
     both_got = along(both_chip, plane[0])
     wide_near = stack(wide_chip, wide_got, deps=(both_chip,))
     wide_far = along(wide_near, plane[1])
-    og_sums, out_saved = run(
+    og_sums, out_saved, out_scale = run(
         functools.partial(out_back, row_total),
         [
             sums_shape(2048),
-            FarOut(shape((264, 2048)), [(0, 64), (128, 64), (64, 64), (192, 72)]),
+            FarOut(shape((256, 2048), BF), [(0, 64), (128, 64), (64, 64), (192, 64)]),
+            FarOut(shape((8, 2048))),
         ],
         (expanded, exp_sums, *far(gain_x, bias_x, wide), Far(cot, other=cot_got)),
         choose=info,
@@ -1159,7 +1162,7 @@
     hg, og_total, *blocks = run(
         functools.partial(expand_back, row_total),
         [shape((128, 512), BF), FarOut(shape((8, 2048)))] + [shape((128, 640), BF)] * 4,
-        (og_sums, Far(out_saved), Far(saved, 136, 128), *far(gain_x, expand_weight)),
+        (og_sums, *far(out_saved, out_scale), Far(saved, 136, 128), *far(gain_x, expand_weight)),
         (info,),
         [pltpu.VMEM((128, 512), BF), pltpu.VMEM((128, 2048), BF)],
         deps=(both_near,),

time: 190 us -> 190 us (level)
  no operation moved by 1% of the time
where the time goes in v1:
time: 190 us; the launch traced here: 189 us
  starting transfers between devices  75.9 us (40%)
  Pallas kernels  55.6 us (29%)
  waiting for transfers between devices  54.9 us (29%)
    ppermute x63, starting transfers between devices, exchange(): return lax.ppermute(value, ALL, route)  75.9 us
    ppermute x63, waiting for transfers between devices, exchange(): return lax.ppermute(value, ALL, route)  54.9 us
    pallas_call x34, Pallas kernels, run(): pl.pallas_call(regrouped, grid_spec=pltpu.PrefetchScalarGridSpec(num_scal...  44.4 us
    pallas_call x3, Pallas kernels, finish(): pl.pallas_call(kernel, grid_spec=pltpu.PrefetchScalarGridSpec(num_scalar_...  9.67 us
  transfers between devices with their start and end apart: 63, of which 30 were waited for; matrix products, arithmetic and copies ran while one was open for 1% of the time, Pallas kernels for 24%

profile of v1, /device:TPU:1, one launch (start us, length us, event | category | flops | bytes accessed | tf_op | source)
XLA Modules:
  0.0 189.2 jit_solution(6093654972959694922)
XLA Ops:
  1.6 4.5 %collective-permute-start = (bf16[208,64]{1,0:T(8,128)(2,1)S(1)}, bf16[208,64]{1,0:T(8,128)(2,1)S(1)}, u32[]{:S(2)}, u32[]{:S(2)}) collective-permute-start(bf16[208,64]{1,0:T(8,128)(2,1)S(1)} %shard_map.306.refs_1_.refs_7_), channel_id=1, source_target_pairs={{1,4},{3,6},{4,1},{6,3},{9,12},{11,14},{12,9},{14,11},{17,20},{19,... | collective-permute-start | bytes 79880 | tf_op jit(solution)/shard_map/ppermute | solution.py:944
  7.9 2.8 %shard_map.307 = (f32[512,512]{1,0:T(8,128)S(1)}, f32[2,512]{1,0:T(2,128)S(1)}) custom-call(s32[6]{0:T(128)S(1)} %stack.27.refs_0_.refs_1_.info, bf16[208,64]{1,0:T(8,128)(2,1)S(1)} %shard_map.306.refs_1_.refs_7_, bf16[208,64]{1,0:T(8,128)(2,1)S(1)} %collective-permute-done.refs_2_.refs_8_, bf16[64,147]{1,0:T(8,128)(2,1)} %bitcast.50, bf16[9,6,64]{2,1,0:T(8,128)(2,1)} %refs_4_.3), custom_call_target="tpu_custom_call" | custom-call | flops 1000000 | bytes 1000000 | tf_op jit(solution)/shard_map/pallas_call | solution.py:921
  14.0 3.6 %collective-permute-start.10 = (bf16[8,2,8,2048]{3,2,1,0:T(8,128)(2,1)}, bf16[8,2,8,2048]{3,2,1,0:T(8,128)(2,1)S(1)}, u32[]{:S(2)}, u32[]{:S(2)}) collective-permute-start(bf16[8,2,8,2048]{3,2,1,0:T(8,128)(2,1)} %shard_map.309.refs_9_), channel_id=1, source_target_pairs={{1,4},{3,6},{4,1},{6,3},{9,12},{11,14},{12,9},{14,11},{17,20},{19,... | collective-permute-start | bytes 1572872 | tf_op jit(solution)/shard_map/ppermute | solution.py:944
  17.6 3.4 %collective-permute-start.2 = (f32[2,512]{1,0:T(2,128)S(1)}, f32[2,512]{1,0:T(2,128)S(1)}, u32[]{:S(2)}, u32[]{:S(2)}) collective-permute-start(f32[2,512]{1,0:T(2,128)S(1)} %add.27.refs_2_), channel_id=1, source_target_pairs={{0,24},{1,25},{2,26},{3,27},{4,28},{5,29},{6,30},{7,31},{8,16},{9,... | collective-permute-start | bytes 12296 | tf_op jit(solution)/shard_map/ppermute | solution.py:944
  24.4 2.8 %shard_map.308 = (bf16[128,2048]{1,0:T(8,128)(2,1)}, bf16[128,1024]{1,0:T(8,128)(2,1)S(1)}, bf16[128,1024]{1,0:T(8,128)(2,1)S(1)}, f32[128,512]{1,0:T(8,128)S(1)...) custom-call(s32[6]{0:T(128)S(1)} %stack.27.refs_0_.refs_1_.info, f32[512,512]{1,0:T(8,128)S(1)} %get-tuple-element.79.refs_1_, ...), custom_call_target="tpu_custom_call" | custom-call | flops 1000000 | bytes 1000000 | tf_op jit(solution)/shard_map/pallas_call | solution.py:921
  35.0 4.5 %shard_map.311 = (bf16[128,512]{1,0:T(8,128)(2,1)S(1)}, bf16[128,512]{1,0:T(8,128)(2,1)S(1)}, f32[128,2048]{1,0:T(8,128)S(1)}, f32[2,2048]{1,0:T(2,128)S(1)}, f32[264,512]{1,0:T(8,128)}) custom-call(s32[6]{0:T(128)S(1)} %stack.27.refs_0_.refs_1_.info, s32[6]{0:T(128)S(1)} %stack.27.refs_0_.refs_1_.info, f32[128,512]{1,0:T(8,128)S(1)} %get-tuple-element.81.refs_2_, ...), custom_call_target="tpu_custom_call" | custom-call | flops 1000000 | bytes 1000000 | tf_op jit(solution)/shard_map/pallas_call | solution.py:921
  50.1 3.3 %shard_map.314 = (f32[2,2048]{1,0:T(2,128)S(1)}, bf16[256,2048]{1,0:T(8,128)(2,1)}, f32[8,2048]{1,0:T(8,128)}) custom-call(s32[6]{0:T(128)S(1)} %stack.27.refs_0_.refs_1_.info, f32[128,2048]{1,0:T(8,128)S(1)} %get-tuple-element.88.refs_1_, f32[2,2048]{1,0:T(2,128)S(1)} %add.29.refs_2_, f32[2,2048]{1,0:T(2,128)S(1)} %collective-permute-done.14.refs_3_, ...), custom_call_target="tpu_custom_call" | custom-call | flops 1000000 | bytes 1000000 | tf_op jit(solution)/shard_map/pallas_call | solution.py:921
  62.9 3.6 %shard_map.316 = (bf16[128,512]{1,0:T(8,128)(2,1)S(1)}, f32[8,2048]{1,0:T(8,128)}, bf16[128,640]{1,0:T(8,128)(2,1)S(1)}, bf16[128,640]{1,0:T(8,128)(2,1)S(1)}, b...) custom-call(s32[6]{0:T(128)S(1)} %stack.27.refs_0_.refs_1_.info, f32[2,2048]{1,0:T(2,128)S(1)} %add.30.refs_2_.refs_1_, ...), custom_call_target="tpu_custom_call" | custom-call | flops 1000000 | bytes 1000000 | tf_op jit(solution)/shard_map/pallas_call | solution.py:921
  69.3 5.3 %shard_map.317 = (f32[128,512]{1,0:T(8,128)S(1)}, f32[2,512]{1,0:T(2,128)S(1)}, f32[256,256]{1,0:T(8,128)S(1)}) custom-call(s32[6]{0:T(128)S(1)} %stack.27.refs_0_.refs_1_.info, bf16[208,64]{1,0:T(8,128)(2,1)} %copy-done.1, bf16[208,64]{1,0:T(8,128)(2,1)} %copy-done.2, bf16[128,512]{1,0:T(8,128)(2,1)S(1)} %get-tuple-element.98.refs_3_, ...), custom_call_target="tpu_custom_call" | custom-call | flops 1000000 | bytes 1000000 | tf_op jit(solution)/shard_map/pallas_call | solution.py:921
  86.3 4.2 %shard_map.320 = (f32[512,512]{1,0:T(8,128)S(1)}, f32[2,512]{1,0:T(2,128)S(1)}, f32[8,512]{1,0:T(8,128)}, bf16[128,256]{1,0:T(8,128)(2,1)S(1)}, bf16[128,256]{1,...) custom-call(s32[6]{0:T(128)S(1)} %stack.27.refs_0_.refs_1_.info, ...), custom_call_target="tpu_custom_call" | custom-call | flops 1000000 | bytes 1000000 | tf_op jit(solution)/shard_map/pallas_call | solution.py:921
  97.4 2.9 %collective-permute-start.36 = (bf16[512,256]{1,0:T(8,128)(2,1)S(1)}, bf16[512,256]{1,0:T(8,128)(2,1)S(1)}, u32[]{:S(2)}, u32[]{:S(2)}) collective-permute-start(bf16[512,256]{1,0:T(8,128)(2,1)S(1)} %shard_map.322.refs_2_.refs_7_), channel_id=1, source_target_pairs={{0,1},{1,0},{2,3},{3,2},{4,5},{5,4},{6,7},{7,6},{8,9},{9,8},{10,11... | collective-permute-start | bytes 786440 | tf_op jit(solution)/shard_map/ppermute | solution.py:944
  104.0 6.3 %collective-permute-done.40.refs_2_ = bf16[576,128]{1,0:T(8,128)(2,1)S(1)} collective-permute-done((bf16[576,128]{1,0:T(8,128)(2,1)S(1)}, bf16[576,128]{1,0:T(8,128)(2,1)S(1)}, u32[]{:S(2)}, u32[]{:S(2)}) %collective-permute-start.40) | collective-permute-done | bytes 147488 | tf_op jit(solution)/shard_map/ppermute | solution.py:944
  115.9 7.9 %collective-permute-done.39.refs_2_ = bf16[1088,128]{1,0:T(8,128)(2,1)S(1)} collective-permute-done((bf16[1088,128]{1,0:T(8,128)(2,1)S(1)}, bf16[1088,128]{1,0:T(8,128)(2,1)S(1)}, u32[]{:S(2)}, u32[]{:S(2)}) %collective-permute-start.39) | collective-permute-done | bytes 278560 | tf_op jit(solution)/shard_map/ppermute | solution.py:944
  126.7 7.1 %shard_map.329 = (f32[8,3,8,64]{3,2,1,0:T(8,128)S(1)}, f32[200,128]{1,0:T(8,128)S(1)}) custom-call(s32[6]{0:T(128)S(1)} %stack.27.refs_0_.refs_1_.info, bf16[208,64]{1,0:T(8,128)(2,1)} %copy-done.1, bf16[208,64]{1,0:T(8,128)(2,1)} %copy-done.2, bf16[64,147]{1,0:T(8,128)(2,1)} %bitcast.51, bf16[9,6,64]{2,1,0:T(8,128)(2,1)} %refs_4_.3, ...), custom_call_target="tpu_custom_call" | custom-call | flops 1000000 | bytes 1000000 | tf_op jit(solution)/shard_map/pallas_call | solution.py:921
  136.6 5.1 %collective-permute-done.46.refs_2_ = bf16[544,128]{1,0:T(8,128)(2,1)S(1)} collective-permute-done((bf16[544,128]{1,0:T(8,128)(2,1)S(1)}, bf16[544,128]{1,0:T(8,128)(2,1)S(1)}, u32[]{:S(2)}, u32[]{:S(2)}) %collective-permute-start.46) | collective-permute-done | bytes 139296 | tf_op jit(solution)/shard_map/ppermute | solution.py:944
  142.4 5.7 %collective-permute-done.48.refs_2_ = bf16[1088,128]{1,0:T(8,128)(2,1)S(1)} collective-permute-done((bf16[1088,128]{1,0:T(8,128)(2,1)S(1)}, bf16[1088,128]{1,0:T(8,128)(2,1)S(1)}, u32[]{:S(2)}, u32[]{:S(2)}) %collective-permute-start.48) | collective-permute-done | bytes 278560 | tf_op jit(solution)/shard_map/ppermute | solution.py:944
  150.3 4.0 %collective-permute-start.50 = (f32[200,128]{1,0:T(8,128)S(1)}, f32[200,128]{1,0:T(8,128)S(1)}, u32[]{:S(2)}, u32[]{:S(2)}) collective-permute-start(f32[200,128]{1,0:T(8,128)S(1)} %get-tuple-element.119.refs_2_.refs_0_), channel_id=1, source_target_pairs={{0,1},{1,0},{2,3},{3,2},{4,5},{5,4},{6,7},{7,6},{8,9},{9,8},{10,11... | collective-permute-start | bytes 307208 | tf_op jit(solution)/shard_map/ppermute | solution.py:944
  156.3 3.2 %collective-permute-done.51.refs_1_ = f32[200,128]{1,0:T(8,128)S(1)} collective-permute-done((f32[200,128]{1,0:T(8,128)S(1)}, f32[200,128]{1,0:T(8,128)S(1)}, u32[]{:S(2)}, u32[]{:S(2)}) %collective-permute-start.51) | collective-permute-done | bytes 102432 | tf_op jit(solution)/shard_map/ppermute | solution.py:944
  159.7 3.2 %collective-permute-start.54 = (bf16[4352,128]{1,0:T(8,128)(2,1)S(1)}, bf16[4352,128]{1,0:T(8,128)(2,1)S(1)}, u32[]{:S(2)}, u32[]{:S(2)}) collective-permute-start(bf16[4352,128]{1,0:T(8,128)(2,1)S(1)} %shard_map.337.rest_0_), channel_id=1, source_target_pairs={{0,1},{1,0},{2,3},{3,2},{4,5},{5,4},{6,7},{7,6},{8,9},{9,8},{10,11... | collective-permute-start | bytes 3342344 | tf_op jit(solution)/shard_map/ppermute | solution.py:944
  164.5 4.3 %shard_map.338 = (f32[9,512,512]{2,1,0:T(8,128)}, f32[8,128]{1,0:T(8,128)S(1)}) custom-call(s32[6]{0:T(128)S(1)} %stack.27.refs_0_.refs_1_.info, bf16[2,2304,128]{2,1,0:T(8,128)(2,1)S(1)} %bitcast.34, bf16[2,2304,128]{2,1,0:T(8,128)(2,1)S(1)} %bitcast.35, bf16[2,2304,128]{2,1,0:T(8,128)(2,1)S(1)} %bitcast.42, bf16[2,2304,128]{2,1,0:T(8,128)(2,1)S(1)} %bitcast.43, ...), custom_call_target="tpu_custom_call" | custom-call | tf_op jit(solution)/shard_map/pallas_call | solution.py:966
  170.8 2.7 %shard_map.340 = (f32[512,2048]{1,0:T(8,128)}, f32[2048,512]{1,0:T(8,128)}, f32[8,128]{1,0:T(8,128)S(1)}) custom-call(s32[6]{0:T(128)S(1)} %stack.27.refs_0_.refs_1_.info, bf16[2,2176,128]{2,1,0:T(8,128)(2,1)S(1)} %bitcast.32, bf16[2,2176,128]{2,1,0:T(8,128)(2,1)S(1)} %bitcast.38, f32[200,128]{1,0:T(8,128)S(1)} %shard_map.339.rest_0_.tail0), custom_call_target="tpu_custom_call" | custom-call | tf_op jit(solution)/shard_map/pallas_call | solution.py:966
  173.5 4.1 %collective-permute-done.53.refs_0_ = bf16[4352,128]{1,0:T(8,128)(2,1)S(1)} collective-permute-done((bf16[4352,128]{1,0:T(8,128)(2,1)S(1)}, bf16[4352,128]{1,0:T(8,128)(2,1)S(1)}, u32[]{:S(2)}, u32[]{:S(2)}) %collective-permute-start.53) | collective-permute-done | bytes 1114144 | tf_op jit(solution)/shard_map/ppermute | solution.py:944
  181.5 3.2 %collective-permute-start.62 = (f32[8,3,8,64]{3,2,1,0:T(8,128)S(1)}, f32[8,3,8,64]{3,2,1,0:T(8,128)S(1)}, u32[]{:S(2)}, u32[]{:S(2)}) collective-permute-start(f32[8,3,8,64]{3,2,1,0:T(8,128)S(1)} %get-tuple-element.122), channel_id=1, source_target_pairs={{0,0},{1,4},{2,2},{3,6},{4,1},{5,5},{6,3},{7,7},{8,8},{9,12},{10,1... | collective-permute-start | bytes 147464 | tf_op jit(solution)/shard_map/ppermute | solution.py:944
  184.8 2.7 %shard_map.342 = (f32[512,2048]{1,0:T(8,128)}, f32[2048,512]{1,0:T(8,128)}, f32[8,128]{1,0:T(8,128)S(1)}) custom-call(s32[6]{0:T(128)S(1)} %stack.27.refs_0_.refs_1_.info, bf16[2,2176,128]{2,1,0:T(8,128)(2,1)S(1)} %bitcast.36, bf16[2,2176,128]{2,1,0:T(8,128)(2,1)S(1)} %bitcast.40, ...), custom_call_target="tpu_custom_call", output_to_operand_aliasing={{0}: (3, {}), {1}: (4, {})} | custom-call | tf_op jit(solution)/shard_map/pallas_call | solution.py:966
  (160 shorter events, 87.4 us)
Async XLA Ops:
  14.0 14.8 %collective-permute-start.10 = (bf16[8,2,8,2048]{3,2,1,0:T(8,128)(2,1)}, bf16[8,2,8,2048]{3,2,1,0:T(8,128)(2,1)S(1)}, u32[]{:S(2)}, u32[]{:S(2)}) collective-permute-start(bf16[8,2,8,2048]{3,2,1,0:T(8,128)(2,1)} %shard_map.309.refs_9_), channel_id=1, source_target_pairs={{1,4},{3,6},{4,1},{6,3},{9,12},{11,14},{12,9},{14,11},{17,20},{19,... | collective-permute-start | bytes 1572872 | tf_op jit(solution)/shard_map/ppermute | solution.py:944
  28.8 13.8 %collective-permute-start.17 = (bf16[256,1024]{1,0:T(8,128)(2,1)S(1)}, bf16[256,1024]{1,0:T(8,128)(2,1)S(1)}, u32[]{:S(2)}, u32[]{:S(2)}) collective-permute-start(bf16[256,1024]{1,0:T(8,128)(2,1)S(1)} %shard_map.310.refs_17_.refs_0_), channel_id=1, source_target_pairs={{0,2},{1,5},{2,0},{3,7},{4,6},{5,1},{6,4},{7,3},{8,10},{9,13},{10,... | collective-permute-start | bytes 1572872 | tf_op jit(solution)/shard_map/ppermute | solution.py:944
  42.7 26.5 %collective-permute-start.26 = (bf16[512,1024]{1,0:T(8,128)(2,1)S(1)}, bf16[512,1024]{1,0:T(8,128)(2,1)S(1)}, u32[]{:S(2)}, u32[]{:S(2)}) collective-permute-start(bf16[512,1024]{1,0:T(8,128)(2,1)S(1)} %shard_map.313.refs_11_.refs_5_), channel_id=1, source_target_pairs={{0,4},{1,3},{2,6},{3,1},{4,0},{5,7},{6,2},{7,5},{8,12},{9,11},{10,... | collective-permute-start | bytes 3145736 | tf_op jit(solution)/shard_map/ppermute | solution.py:944
  43.1 13.4 %collective-permute-start.13 = (bf16[256,512]{1,0:T(8,128)(2,1)S(1)}, bf16[256,512]{1,0:T(8,128)(2,1)S(1)}, u32[]{:S(2)}, u32[]{:S(2)}) collective-permute-start(bf16[256,512]{1,0:T(8,128)(2,1)S(1)} %shard_map.312.refs_2_.refs_0_), channel_id=1, source_target_pairs={{0,2},{1,5},{2,0},{3,7},{4,6},{5,1},{6,4},{7,3},{8,10},{9,13},{10,... | collective-permute-start | bytes 786440 | tf_op jit(solution)/shard_map/ppermute | solution.py:944
  56.6 12.7 %collective-permute-start.19 = (bf16[512,512]{1,0:T(8,128)(2,1)S(1)}, bf16[512,512]{1,0:T(8,128)(2,1)S(1)}, u32[]{:S(2)}, u32[]{:S(2)}) collective-permute-start(bf16[512,512]{1,0:T(8,128)(2,1)S(1)} %shard_map.315.refs_10_.refs_1_), channel_id=1, source_target_pairs={{0,4},{1,3},{2,6},{3,1},{4,0},{5,7},{6,2},{7,5},{8,12},{9,11},{10,... | collective-permute-start | bytes 1572872 | tf_op jit(solution)/shard_map/ppermute | solution.py:944
  66.6 10.8 %collective-permute-start.23 = (bf16[128,640]{1,0:T(8,128)(2,1)S(1)}, bf16[128,640]{1,0:T(8,128)(2,1)S(1)}, u32[]{:S(2)}, u32[]{:S(2)}) collective-permute-start(bf16[128,640]{1,0:T(8,128)(2,1)S(1)} %get-tuple-element.95), channel_id=1, source_target_pairs={{0,2},{1,5},{2,0},{3,7},{4,6},{5,1},{6,4},{7,3},{8,10},{9,13},{10,... | collective-permute-start | bytes 491528 | tf_op jit(solution)/shard_map/ppermute | solution.py:944
  66.6 10.7 %collective-permute-start.24 = (bf16[128,640]{1,0:T(8,128)(2,1)S(1)}, bf16[128,640]{1,0:T(8,128)(2,1)S(1)}, u32[]{:S(2)}, u32[]{:S(2)}) collective-permute-start(bf16[128,640]{1,0:T(8,128)(2,1)S(1)} %get-tuple-element.96), channel_id=1, source_target_pairs={{0,4},{1,3},{2,6},{3,1},{4,0},{5,7},{6,2},{7,5},{8,12},{9,11},{10,... | collective-permute-start | bytes 491528 | tf_op jit(solution)/shard_map/ppermute | solution.py:944
  67.0 10.3 %collective-permute-start.25 = (bf16[128,640]{1,0:T(8,128)(2,1)S(1)}, bf16[128,640]{1,0:T(8,128)(2,1)S(1)}, u32[]{:S(2)}, u32[]{:S(2)}) collective-permute-start(bf16[128,640]{1,0:T(8,128)(2,1)S(1)} %get-tuple-element.97), channel_id=1, source_target_pairs={{0,6},{1,7},{2,4},{3,5},{4,2},{5,3},{6,0},{7,1},{8,14},{9,15},{10,... | collective-permute-start | bytes 491528 | tf_op jit(solution)/shard_map/ppermute | solution.py:944
  85.6 7.7 %collective-permute-start.35 = (bf16[1152,128]{1,0:T(8,128)(2,1)S(1)}, bf16[1152,128]{1,0:T(8,128)(2,1)S(1)}, u32[]{:S(2)}, u32[]{:S(2)}) collective-permute-start(bf16[1152,128]{1,0:T(8,128)(2,1)S(1)} %get-tuple-element.108), channel_id=1, source_target_pairs={{0,8},{1,9},{2,10},{3,11},{4,12},{5,13},{6,14},{7,15},{8,0},{9,1},... | collective-permute-start | bytes 884744 | tf_op jit(solution)/shard_map/ppermute | solution.py:944
  101.5 8.8 %collective-permute-start.40 = (bf16[576,128]{1,0:T(8,128)(2,1)S(1)}, bf16[576,128]{1,0:T(8,128)(2,1)S(1)}, u32[]{:S(2)}, u32[]{:S(2)}) collective-permute-start(bf16[576,128]{1,0:T(8,128)(2,1)S(1)} %shard_map.324.refs_9_.refs_1_), channel_id=1, source_target_pairs={{0,16},{1,17},{2,18},{3,19},{4,20},{5,21},{6,22},{7,23},{8,24},{9,... | collective-permute-start | bytes 442376 | tf_op jit(solution)/shard_map/ppermute | solution.py:944
  110.8 13.9 %collective-permute-start.45 = (bf16[1152,128]{1,0:T(8,128)(2,1)S(1)}, bf16[1152,128]{1,0:T(8,128)(2,1)S(1)}, u32[]{:S(2)}, u32[]{:S(2)}) collective-permute-start(bf16[1152,128]{1,0:T(8,128)(2,1)S(1)} %shard_map.326.refs_3_.refs_1_), channel_id=1, source_target_pairs={{0,8},{1,9},{2,10},{3,11},{4,12},{5,13},{6,14},{7,15},{8,0},{9,1},... | collective-permute-start | bytes 884744 | tf_op jit(solution)/shard_map/ppermute | solution.py:944
  110.9 12.9 %collective-permute-start.39 = (bf16[1088,128]{1,0:T(8,128)(2,1)S(1)}, bf16[1088,128]{1,0:T(8,128)(2,1)S(1)}, u32[]{:S(2)}, u32[]{:S(2)}) collective-permute-start(bf16[1088,128]{1,0:T(8,128)(2,1)S(1)} %get-tuple-element.114), channel_id=1, source_target_pairs={{0,8},{1,9},{2,10},{3,11},{4,12},{5,13},{6,14},{7,15},{8,0},{9,1},... | collective-permute-start | bytes 835592 | tf_op jit(solution)/shard_map/ppermute | solution.py:944
  112.4 12.4 %collective-permute-start.42 = (f32[2,512]{1,0:T(2,128)S(1)}, f32[2,512]{1,0:T(2,128)S(1)}, u32[]{:S(2)}, u32[]{:S(2)}) collective-permute-start(f32[2,512]{1,0:T(2,128)S(1)} %shard_map.323.refs_2_.refs_4_.refs_8_), channel_id=1, source_target_pairs={{0,24},{1,25},{2,26},{3,27},{4,28},{5,29},{6,30},{7,31},{8,16},{9,... | collective-permute-start | bytes 12296 | tf_op jit(solution)/shard_map/ppermute | solution.py:944
  114.4 10.3 %collective-permute-start.43 = (f32[2,512]{1,0:T(2,128)S(1)}, f32[2,512]{1,0:T(2,128)S(1)}, u32[]{:S(2)}, u32[]{:S(2)}) collective-permute-start(f32[2,512]{1,0:T(2,128)S(1)} %shard_map.323.refs_2_.refs_4_.refs_8_), channel_id=1, source_target_pairs={{0,16},{1,17},{2,18},{3,19},{4,20},{5,21},{6,22},{7,23},{8,24},{9,... | collective-permute-start | bytes 12296 | tf_op jit(solution)/shard_map/ppermute | solution.py:944
  114.4 10.3 %collective-permute-start.44 = (f32[2,512]{1,0:T(2,128)S(1)}, f32[2,512]{1,0:T(2,128)S(1)}, u32[]{:S(2)}, u32[]{:S(2)}) collective-permute-start(f32[2,512]{1,0:T(2,128)S(1)} %shard_map.323.refs_2_.refs_4_.refs_8_), channel_id=1, source_target_pairs={{0,8},{1,9},{2,10},{3,11},{4,12},{5,13},{6,14},{7,15},{8,0},{9,1},... | collective-permute-start | bytes 12296 | tf_op jit(solution)/shard_map/ppermute | solution.py:944
  125.3 9.1 %collective-permute-start.47 = (bf16[2304,128]{1,0:T(8,128)(2,1)S(1)}, bf16[2304,128]{1,0:T(8,128)(2,1)S(1)}, u32[]{:S(2)}, u32[]{:S(2)}) collective-permute-start(bf16[2304,128]{1,0:T(8,128)(2,1)S(1)} %shard_map.328.refs_14_.refs_0_), channel_id=1, source_target_pairs={{0,4},{1,3},{2,6},{3,1},{4,0},{5,7},{6,2},{7,5},{8,12},{9,11},{10,... | collective-permute-start | bytes 1769480 | tf_op jit(solution)/shard_map/ppermute | solution.py:944
  125.4 8.4 %collective-permute-start.41 = (bf16[544,128]{1,0:T(8,128)(2,1)S(1)}, bf16[544,128]{1,0:T(8,128)(2,1)S(1)}, u32[]{:S(2)}, u32[]{:S(2)}) collective-permute-start(bf16[544,128]{1,0:T(8,128)(2,1)S(1)} %get-tuple-element.116), channel_id=1, source_target_pairs={{0,16},{1,17},{2,18},{3,19},{4,20},{5,21},{6,22},{7,23},{8,24},{9,... | collective-permute-start | bytes 417800 | tf_op jit(solution)/shard_map/ppermute | solution.py:944
  134.5 21.3 %collective-permute-start.52 = (bf16[4608,128]{1,0:T(8,128)(2,1)S(1)}, bf16[4608,128]{1,0:T(8,128)(2,1)S(1)}, u32[]{:S(2)}, u32[]{:S(2)}) collective-permute-start(bf16[4608,128]{1,0:T(8,128)(2,1)S(1)} %shard_map.331.refs_3_), channel_id=1, source_target_pairs={{0,2},{1,5},{2,0},{3,7},{4,6},{5,1},{6,4},{7,3},{8,10},{9,13},{10,... | collective-permute-start | bytes 3538952 | tf_op jit(solution)/shard_map/ppermute | solution.py:944
  148.6 11.0 %collective-permute-start.49 = (bf16[2176,128]{1,0:T(8,128)(2,1)S(1)}, bf16[2176,128]{1,0:T(8,128)(2,1)S(1)}, u32[]{:S(2)}, u32[]{:S(2)}) collective-permute-start(bf16[2176,128]{1,0:T(8,128)(2,1)S(1)} %shard_map.333.refs_2_.refs_0_), channel_id=1, source_target_pairs={{0,4},{1,3},{2,6},{3,1},{4,0},{5,7},{6,2},{7,5},{8,12},{9,11},{10,... | collective-permute-start | bytes 1671176 | tf_op jit(solution)/shard_map/ppermute | solution.py:944
  155.4 9.1 %collective-permute-start.56 = (bf16[4608,128]{1,0:T(8,128)(2,1)S(1)}, bf16[4608,128]{1,0:T(8,128)(2,1)S(1)}, u32[]{:S(2)}, u32[]{:S(2)}) collective-permute-start(bf16[4608,128]{1,0:T(8,128)(2,1)S(1)} %shard_map.331.refs_3_), channel_id=1, source_target_pairs={{0,1},{1,0},{2,3},{3,2},{4,5},{5,4},{6,7},{7,6},{8,9},{9,8},{10,11... | collective-permute-start | bytes 3538952 | tf_op jit(solution)/shard_map/ppermute | solution.py:944
  155.9 8.6 %collective-permute-start.57 = (bf16[4608,128]{1,0:T(8,128)(2,1)S(1)}, bf16[4608,128]{1,0:T(8,128)(2,1)S(1)}, u32[]{:S(2)}, u32[]{:S(2)}) collective-permute-start(bf16[4608,128]{1,0:T(8,128)(2,1)S(1)} %shard_map.335.refs_2_), channel_id=1, source_target_pairs={{0,1},{1,0},{2,3},{3,2},{4,5},{5,4},{6,7},{7,6},{8,9},{9,8},{10,11... | collective-permute-start | bytes 3538952 | tf_op jit(solution)/shard_map/ppermute | solution.py:944
  159.7 11.0 %collective-permute-start.54 = (bf16[4352,128]{1,0:T(8,128)(2,1)S(1)}, bf16[4352,128]{1,0:T(8,128)(2,1)S(1)}, u32[]{:S(2)}, u32[]{:S(2)}) collective-permute-start(bf16[4352,128]{1,0:T(8,128)(2,1)S(1)} %shard_map.337.rest_0_), channel_id=1, source_target_pairs={{0,1},{1,0},{2,3},{3,2},{4,5},{5,4},{6,7},{7,6},{8,9},{9,8},{10,11... | collective-permute-start | bytes 3342344 | tf_op jit(solution)/shard_map/ppermute | solution.py:944
  162.9 14.6 %collective-permute-start.53 = (bf16[4352,128]{1,0:T(8,128)(2,1)S(1)}, bf16[4352,128]{1,0:T(8,128)(2,1)S(1)}, u32[]{:S(2)}, u32[]{:S(2)}) collective-permute-start(bf16[4352,128]{1,0:T(8,128)(2,1)S(1)} %shard_map.337.rest_0_), channel_id=1, source_target_pairs={{0,2},{1,5},{2,0},{3,7},{4,6},{5,1},{6,4},{7,3},{8,10},{9,13},{10,... | collective-permute-start | bytes 3342344 | tf_op jit(solution)/shard_map/ppermute | solution.py:944
  178.7 8.8 %collective-permute-start.59 = (f32[200,128]{1,0:T(8,128)S(1)}, f32[200,128]{1,0:T(8,128)S(1)}, u32[]{:S(2)}, u32[]{:S(2)}) collective-permute-start(f32[200,128]{1,0:T(8,128)S(1)} %shard_map.339.rest_0_.tail0), channel_id=1, source_target_pairs={{0,6},{1,7},{2,4},{3,5},{4,2},{5,3},{6,0},{7,1},{8,14},{9,15},{10,... | collective-permute-start | bytes 307208 | tf_op jit(solution)/shard_map/ppermute | solution.py:944
  (44 other events, 212.0 us)
